TPU v7x, 32 devices: a whole 2x2x4 slice. The times are simulated.
32 devices in a mesh: batch: 16 (over z, y, x), rows: 2 (over core).
Axes of the slice: x: 2, y: 2, z: 4, core: 2. Of those that a mesh axis runs over, the one named last changes fastest.
Arguments:
- images: bfloat16 [2, 16, 64, 16, 1024], P(None, 'rows', 'batch'), may hold values from -6 to 6
- crop_sizes: int32 [2, 64], replicated, may hold values from 8 to 16, as said below
- reduce_a: bfloat16 [1024, 512], replicated, may hold values from -0.1875 to 0.1875
- reduce_gain_a: float32 [512], replicated, may hold values from 0.25 to 1.75
- reduce_bias_a: float32 [512], replicated, may hold values from -2 to 2
- spatial_a: bfloat16 [4608, 512], replicated, may hold values from -0.09375 to 0.09375
- spatial_gain_a: float32 [512], replicated, may hold values from 0.25 to 1.75
- spatial_bias_a: float32 [512], replicated, may hold values from -2 to 2
- expand_a: bfloat16 [512, 2048], replicated, may hold values from -0.25 to 0.25
- expand_gain_a: float32 [2048], P('rows'), may hold values from 0.25 to 1.75
- expand_bias_a: float32 [2048], P('rows'), may hold values from -2 to 2
- project_a: bfloat16 [1024, 2048], replicated, may hold values from -0.1875 to 0.1875
- project_gain_a: float32 [2048], P('rows'), may hold values from 0.25 to 1.75
- project_bias_a: float32 [2048], P('rows'), may hold values from -2 to 2
- squeeze_a: bfloat16 [2048, 128], P('rows'), may hold values from -0.25 to 0.25
- squeeze_bias_a: float32 [128], replicated, may hold values from -2.5 to 2.5
- excite_a: bfloat16 [128, 2048], P(None, 'rows'), may hold values from -1 to 1
- excite_bias_a: float32 [2048], P('rows'), may hold values from -4 to 4
- reduce_b: bfloat16 [2048, 512], P('rows'), may hold values from -0.125 to 0.125
- reduce_gain_b: float32 [512], replicated, may hold values from 0.25 to 1.75
- reduce_bias_b: float32 [512], replicated, may hold values from -2 to 2
- spatial_b: bfloat16 [4608, 512], replicated, may hold values from -0.09375 to 0.09375
- spatial_gain_b: float32 [512], replicated, may hold values from 0.25 to 1.75
- spatial_bias_b: float32 [512], replicated, may hold values from -2 to 2
- expand_b: bfloat16 [512, 2048], replicated, may hold values from -0.25 to 0.25
- expand_gain_b: float32 [2048], P('rows'), may hold values from 0.25 to 1.75
- expand_bias_b: float32 [2048], P('rows'), may hold values from -2 to 2
- squeeze_b: bfloat16 [2048, 128], P('rows'), may hold values from -0.25 to 0.25
- squeeze_bias_b: float32 [128], replicated, may hold values from -2.5 to 2.5
- excite_b: bfloat16 [128, 2048], P(None, 'rows'), may hold values from -1 to 1
- excite_bias_b: float32 [2048], P('rows'), may hold values from -4 to 4
- cotangent: bfloat16 [2, 8, 64, 8, 2048], P(None, None, 'batch', None, 'rows'), may hold values from -6 to 6
Outputs:
- block_out: bfloat16 [2, 8, 64, 8, 2048], P(None, None, 'batch', None, 'rows')
- images_grad: float32 [2, 16, 64, 16, 1024], P(None, 'rows', 'batch')
- grad_reduce_a: float32 [524288], P(('batch', 'rows'))
- grad_reduce_gain_a: float32 [512], replicated
- grad_reduce_bias_a: float32 [512], replicated
- grad_spatial_a: float32 [2359296], P(('batch', 'rows'))
- grad_spatial_gain_a: float32 [512], replicated
- grad_spatial_bias_a: float32 [512], replicated
- grad_expand_a: float32 [1048576], P(('batch', 'rows'))
- grad_expand_gain_a: float32 [2048], P('rows')
- grad_expand_bias_a: float32 [2048], P('rows')
- grad_project_a: float32 [2097152], P(('batch', 'rows'))
- grad_project_gain_a: float32 [2048], P('rows')
- grad_project_bias_a: float32 [2048], P('rows')
- grad_squeeze_a: float32 [2048, 128], P('rows')
- grad_squeeze_bias_a: float32 [128], replicated
- grad_excite_a: float32 [128, 2048], P(None, 'rows')
- grad_excite_bias_a: float32 [2048], P('rows')
- grad_reduce_b: float32 [2048, 512], P('rows')
- grad_reduce_gain_b: float32 [512], replicated
- grad_reduce_bias_b: float32 [512], replicated
- grad_spatial_b: float32 [2359296], P(('batch', 'rows'))
- grad_spatial_gain_b: float32 [512], replicated
- grad_spatial_bias_b: float32 [512], replicated
- grad_expand_b: float32 [1048576], P(('batch', 'rows'))
- grad_expand_gain_b: float32 [2048], P('rows')
- grad_expand_bias_b: float32 [2048], P('rows')
- grad_squeeze_b: float32 [2048, 128], P('rows')
- grad_squeeze_bias_b: float32 [128], replicated
- grad_excite_b: float32 [128, 2048], P(None, 'rows')
- grad_excite_bias_b: float32 [2048], P('rows')
Inputs may be any that keep to these rules, and one draw needn't show every extreme that they name: crop_sizes[m, b] is the live side of image b's map in micro-batch m, either 16 or 8; both occur in every micro-batch.
All inputs are finite; a program needn't handle non-finite values.
Results may differ from a plain program's by a relative error of at most 0.025.
Values may be sent and summed in bfloat16 or wider, within the bound.
No kernel may reach another device: no remote copies, remote signals or barrier semaphores. Data moves between devices by JAX's collectives and lax.ppermute only.
A program may use at most 256 MiB of HBM per device.

v0:
```python
import math

import jax
import jax.numpy as jnp
from jax import lax
from jax.sharding import PartitionSpec as P

epsilon = 1e-05
HIGHEST = lax.Precision.HIGHEST


def passed_along(block, axis, distance):
    devices = range(lax.axis_size(axis))
    route = [(i - distance, i) for i in devices if i - distance in devices]
    return lax.ppermute(block, axis, route)


def extended_2(array, sides, width):
    for axis, dim in sides:
        size, length = (lax.axis_size(axis), array.shape[dim])
        up = [(i, (i + 1) % size) for i in range(size - 1)]
        down = [(j, i) for i, j in up]
        last = lax.slice_in_dim(array, length - width, length, axis=dim)
        first = lax.slice_in_dim(array, 0, width, axis=dim)
        before = lax.ppermute(last, axis, up)
        after = lax.ppermute(first, axis, down)
        array = jnp.concatenate([before, array, after], axis=dim)
    return array


def silu_slope(values):
    sigma = jax.nn.sigmoid(values)
    return sigma * (1.0 + values * (1.0 - sigma))


def live_mask(limits, first_row, count_rows, width):
    places_rows = first_row + jnp.arange(count_rows, dtype=jnp.int32)
    places_cols = jnp.arange(width, dtype=jnp.int32)
    inside = (places_rows[:, None, None] < limits[None, :, None]) & (
        places_cols[None, None, :] < limits[None, :, None]
    )
    return inside.astype(jnp.float32)[..., None]


def forward_dot(inputs, weight):
    return jnp.dot(inputs, weight, preferred_element_type=jnp.float32)


def input_dot(grads, weight):
    return lax.dot_general(
        grads, weight, (((grads.ndim - 1,), (1,)), ((), ())), preferred_element_type=jnp.float32
    )


def weight_dot(inputs, grads):
    leading = tuple(range(inputs.ndim - 1))
    return lax.dot_general(
        inputs, grads, ((leading, leading), ((), ())), preferred_element_type=jnp.float32
    )


def gather_taps(extended, stride, out_rows, out_cols):
    padded = jnp.pad(extended, ((0, 0), (0, 0), (1, 1), (0, 0)))
    return jnp.concatenate(
        [
            padded[
                row_tap : row_tap + stride * out_rows : stride,
                :,
                col_tap : col_tap + stride * out_cols : stride,
                :,
            ]
            for row_tap in range(3)
            for col_tap in range(3)
        ],
        axis=3,
    )


def spread_taps(grad_patches, extended, stride, out_rows, out_cols):

    def build(fields):
        return gather_taps(fields, stride, out_rows, out_cols)

    pullback = jax.vjp(build, jnp.zeros(extended.shape, jnp.float32))[1]
    return pullback(grad_patches)[0]


def pixel_total(first, second):
    return lax.psum((first, second), ("batch", "rows"))


def channel_total(first, second):
    return lax.psum((first, second), "batch")


def gate_total(partial_value):
    return lax.psum(partial_value, "rows")


def norm_forward(values, inside, counted, gain_term, bias_term, reducer):
    linear, squares = reducer(
        jnp.sum(values * inside, axis=(0, 1, 2)), jnp.sum(values * values * inside, axis=(0, 1, 2))
    )
    centre = linear / counted
    inverse = lax.rsqrt(squares / counted - centre * centre + epsilon)
    scaled = (values - centre) * inverse
    return ((scaled * gain_term + bias_term) * inside, scaled, inverse)


def norm_backward(grads, inside, counted, gain_term, scaled, inverse, reducer):
    live_grad = grads * inside
    bias_grad, gain_grad = reducer(
        jnp.sum(live_grad, axis=(0, 1, 2)), jnp.sum(live_grad * scaled, axis=(0, 1, 2))
    )
    value_grad = (
        (live_grad - (bias_grad + scaled * gain_grad) / counted) * (gain_term * inverse) * inside
    )
    return (value_grad, gain_grad, bias_grad)


def excite_forward(normed, pixel_count, squeeze, squeeze_bias, excite, excite_bias):
    pooled = jnp.sum(normed, axis=(0, 2)) / pixel_count[:, None]
    partial_value = jnp.dot(pooled, squeeze.astype(jnp.float32), precision=HIGHEST)
    inner = gate_total(partial_value) + squeeze_bias
    hidden = jax.nn.silu(inner)
    gating = jax.nn.sigmoid(
        jnp.dot(hidden, excite.astype(jnp.float32), precision=HIGHEST) + excite_bias
    )
    return (gating, (pooled, inner, hidden))


def excite_backward(gate_grad, gating, cache, pixel_count, squeeze, excite):
    pooled, inner, hidden = cache
    logit_grad = gate_grad * gating * (1.0 - gating)
    excite_grad = jnp.dot(hidden.T, logit_grad, precision=HIGHEST)
    excite_bias_grad = jnp.sum(logit_grad, axis=0)
    hidden_grad = gate_total(jnp.dot(logit_grad, excite.astype(jnp.float32).T, precision=HIGHEST))
    inner_grad = hidden_grad * silu_slope(inner)
    squeeze_grad = jnp.dot(pooled.T, inner_grad, precision=HIGHEST)
    squeeze_bias_grad = jnp.sum(inner_grad, axis=0)
    pooled_grad = jnp.dot(inner_grad, squeeze.astype(jnp.float32).T, precision=HIGHEST)
    return (
        pooled_grad / pixel_count[:, None],
        (squeeze_grad, squeeze_bias_grad, excite_grad, excite_bias_grad),
    )


def accumulate(totals, label, addend):
    totals[label] = totals.get(label, 0.0) + addend


def add_terms(running, addend):
    if running is None:
        return addend
    return tuple((left + right for left, right in zip(running, addend)))


def unpack(flat, targets):
    pieces = []
    offset = 0
    for target in targets:
        length = math.prod(target)
        pieces.append(flat[offset : offset + length].reshape(target))
        offset += length
    return pieces


def per_device(
    images,
    crop_sizes,
    reduce_a,
    reduce_gain_a,
    reduce_bias_a,
    spatial_a,
    spatial_gain_a,
    spatial_bias_a,
    expand_a,
    expand_gain_a,
    expand_bias_a,
    project_a,
    project_gain_a,
    project_bias_a,
    squeeze_a,
    squeeze_bias_a,
    excite_a,
    excite_bias_a,
    reduce_b,
    reduce_gain_b,
    reduce_bias_b,
    spatial_b,
    spatial_gain_b,
    spatial_bias_b,
    expand_b,
    expand_gain_b,
    expand_bias_b,
    squeeze_b,
    squeeze_bias_b,
    excite_b,
    excite_bias_b,
    cotangent,
):
    micro_count = images.shape[0]
    fine_rows = images.shape[1]
    batch_local = images.shape[2]
    full_side = images.shape[3]
    half_side = full_side // 2
    coarse_rows = fine_rows // 2
    split_rows = half_side // lax.axis_size("rows")
    row_index = lax.axis_index("rows")
    batch_index = lax.axis_index("batch")
    totals = {}
    outputs = []
    input_grads = []
    early_sums = None
    late_sums = None
    for micro in range(micro_count):
        crop_all = crop_sizes[micro]
        crop_local = lax.dynamic_slice_in_dim(crop_all, batch_index * batch_local, batch_local)
        half_all = crop_all // 2
        half_local = crop_local // 2
        count_fine = jnp.sum(crop_all * crop_all).astype(jnp.float32)
        count_coarse = jnp.sum(half_all * half_all).astype(jnp.float32)
        pixel_count = (half_local * half_local).astype(jnp.float32)
        mask_fine = live_mask(crop_local, row_index * fine_rows, fine_rows, full_side)
        mask_coarse = live_mask(half_local, row_index * coarse_rows, coarse_rows, half_side)
        mask_channel = live_mask(half_local, 0, half_side, half_side)
        mask_split = live_mask(half_local, row_index * split_rows, split_rows, half_side)
        source = images[micro]
        conv_one = forward_dot(source, reduce_a)
        normed_one, scaled_one, inverse_one = norm_forward(
            conv_one, mask_fine, count_fine, reduce_gain_a, reduce_bias_a, pixel_total
        )
        active_one = jax.nn.silu(normed_one).astype(jnp.bfloat16)
        above_row = passed_along(active_one[-1:], "rows", 1)
        extended_one = jnp.concatenate([above_row, active_one], axis=0)
        patches_one = gather_taps(extended_one, 2, coarse_rows, half_side)
        conv_two = forward_dot(patches_one, spatial_a)
        normed_two, scaled_two, inverse_two = norm_forward(
            conv_two, mask_coarse, count_coarse, spatial_gain_a, spatial_bias_a, pixel_total
        )
        active_two = jax.nn.silu(normed_two).astype(jnp.bfloat16)
        expanded = forward_dot(active_two, expand_a).astype(jnp.bfloat16)
        strided = source[::2, :, ::2, :]
        projected = forward_dot(strided, project_a).astype(jnp.bfloat16)
        expanded_owned, projected_owned = (
            lax.all_to_all(expanded, "rows", split_axis=3, concat_axis=0, tiled=True),
            lax.all_to_all(projected, "rows", split_axis=3, concat_axis=0, tiled=True),
        )
        normed_three, scaled_three, inverse_three = norm_forward(
            expanded_owned.astype(jnp.float32),
            mask_channel,
            count_coarse,
            expand_gain_a,
            expand_bias_a,
            channel_total,
        )
        normed_side, scaled_side, inverse_side = norm_forward(
            projected_owned.astype(jnp.float32),
            mask_channel,
            count_coarse,
            project_gain_a,
            project_bias_a,
            channel_total,
        )
        gate_one, cache_one = excite_forward(
            normed_three, pixel_count, squeeze_a, squeeze_bias_a, excite_a, excite_bias_a
        )
        summed_one = normed_three * gate_one[None, :, None, :] + normed_side
        middle = jax.nn.silu(summed_one).astype(jnp.bfloat16)
        conv_four = lax.psum_scatter(
            forward_dot(middle, reduce_b).astype(jnp.bfloat16),
            "rows",
            scatter_dimension=0,
            tiled=True,
        ).astype(jnp.float32)
        normed_four, scaled_four, inverse_four = norm_forward(
            conv_four, mask_split, count_coarse, reduce_gain_b, reduce_bias_b, pixel_total
        )
        active_four = jax.nn.silu(normed_four).astype(jnp.bfloat16)
        extended_four = extended_2(active_four, (("rows", 0),), 1)
        patches_four = gather_taps(extended_four, 1, split_rows, half_side)
        conv_five = forward_dot(patches_four, spatial_b)
        normed_five, scaled_five, inverse_five = norm_forward(
            conv_five, mask_split, count_coarse, spatial_gain_b, spatial_bias_b, pixel_total
        )
        active_five = jax.nn.silu(normed_five).astype(jnp.bfloat16)
        expanded_b = forward_dot(active_five, expand_b).astype(jnp.bfloat16)
        expanded_b_owned = lax.all_to_all(
            expanded_b, "rows", split_axis=3, concat_axis=0, tiled=True
        )
        normed_six, scaled_six, inverse_six = norm_forward(
            expanded_b_owned.astype(jnp.float32),
            mask_channel,
            count_coarse,
            expand_gain_b,
            expand_bias_b,
            channel_total,
        )
        gate_two, cache_two = excite_forward(
            normed_six, pixel_count, squeeze_b, squeeze_bias_b, excite_b, excite_bias_b
        )
        summed_two = normed_six * gate_two[None, :, None, :] + middle.astype(jnp.float32)
        outputs.append(jax.nn.silu(summed_two).astype(jnp.bfloat16))
        upstream = cotangent[micro].astype(jnp.float32)
        grad_summed_two = upstream * silu_slope(summed_two)
        gate_grad_two = jnp.sum(grad_summed_two * normed_six, axis=(0, 2))
        pooled_two, excite_grads_two = excite_backward(
            gate_grad_two, gate_two, cache_two, pixel_count, squeeze_b, excite_b
        )
        accumulate(totals, "squeeze_b", excite_grads_two[0])
        accumulate(totals, "squeeze_bias_b", excite_grads_two[1])
        accumulate(totals, "excite_b", excite_grads_two[2])
        accumulate(totals, "excite_bias_b", excite_grads_two[3])
        grad_normed_six = (
            grad_summed_two * gate_two[None, :, None, :] + pooled_two[None, :, None, :]
        )
        grad_conv_six, gain_six, bias_six = norm_backward(
            grad_normed_six,
            mask_channel,
            count_coarse,
            expand_gain_b,
            scaled_six,
            inverse_six,
            channel_total,
        )
        accumulate(totals, "expand_gain_b", gain_six)
        accumulate(totals, "expand_bias_b", bias_six)
        back_six = lax.all_to_all(
            grad_conv_six.astype(jnp.bfloat16), "rows", split_axis=0, concat_axis=3, tiled=True
        )
        wide_expand_b = weight_dot(active_five, back_six)
        grad_active_five = input_dot(back_six, expand_b)
        grad_conv_five, gain_five, bias_five = norm_backward(
            grad_active_five * silu_slope(normed_five),
            mask_split,
            count_coarse,
            spatial_gain_b,
            scaled_five,
            inverse_five,
            pixel_total,
        )
        accumulate(totals, "spatial_gain_b", gain_five)
        accumulate(totals, "spatial_bias_b", bias_five)
        rounded_five = grad_conv_five.astype(jnp.bfloat16)
        wide_spatial_b = weight_dot(patches_four, rounded_five)
        late_sums = add_terms(late_sums, (wide_spatial_b.reshape(-1), wide_expand_b.reshape(-1)))
        grad_extended_four = spread_taps(
            input_dot(rounded_five, spatial_b), extended_four, 1, split_rows, half_side
        )
        edge_rows = jnp.concatenate([grad_extended_four[:1], grad_extended_four[-1:]], axis=0)
        arrived = extended_2(edge_rows.astype(jnp.bfloat16), (("rows", 0),), 1).astype(
            edge_rows.dtype
        )
        grad_active_four = grad_extended_four[1:-1]
        grad_active_four = grad_active_four.at[0].add(arrived[0]).at[-1].add(arrived[-1])
        grad_conv_four, gain_four, bias_four = norm_backward(
            grad_active_four * silu_slope(normed_four),
            mask_split,
            count_coarse,
            reduce_gain_b,
            scaled_four,
            inverse_four,
            pixel_total,
        )
        accumulate(totals, "reduce_gain_b", gain_four)
        accumulate(totals, "reduce_bias_b", bias_four)
        rounded_four = grad_conv_four.astype(jnp.bfloat16)
        piece = lax.all_gather(rounded_four, "rows", axis=0, tiled=True)
        grad_inputs = input_dot(piece, reduce_b)
        grad_middle = grad_inputs
        grad_reduce_local = weight_dot(middle, piece)
        accumulate(totals, "reduce_b", grad_reduce_local)
        grad_middle = grad_middle + grad_summed_two
        grad_summed_one = grad_middle * silu_slope(summed_one)
        gate_grad_one = jnp.sum(grad_summed_one * normed_three, axis=(0, 2))
        pooled_one, excite_grads_one = excite_backward(
            gate_grad_one, gate_one, cache_one, pixel_count, squeeze_a, excite_a
        )
        accumulate(totals, "squeeze_a", excite_grads_one[0])
        accumulate(totals, "squeeze_bias_a", excite_grads_one[1])
        accumulate(totals, "excite_a", excite_grads_one[2])
        accumulate(totals, "excite_bias_a", excite_grads_one[3])
        grad_normed_three = (
            grad_summed_one * gate_one[None, :, None, :] + pooled_one[None, :, None, :]
        )
        grad_conv_three, gain_three, bias_three = norm_backward(
            grad_normed_three,
            mask_channel,
            count_coarse,
            expand_gain_a,
            scaled_three,
            inverse_three,
            channel_total,
        )
        grad_conv_side, gain_side, bias_side = norm_backward(
            grad_summed_one,
            mask_channel,
            count_coarse,
            project_gain_a,
            scaled_side,
            inverse_side,
            channel_total,
        )
        accumulate(totals, "expand_gain_a", gain_three)
        accumulate(totals, "expand_bias_a", bias_three)
        accumulate(totals, "project_gain_a", gain_side)
        accumulate(totals, "project_bias_a", bias_side)
        back_three, back_side = (
            lax.all_to_all(
                grad_conv_three.astype(jnp.bfloat16),
                "rows",
                split_axis=0,
                concat_axis=3,
                tiled=True,
            ),
            lax.all_to_all(
                grad_conv_side.astype(jnp.bfloat16), "rows", split_axis=0, concat_axis=3, tiled=True
            ),
        )
        wide_expand_a = weight_dot(active_two, back_three)
        wide_project_a = weight_dot(strided, back_side)
        grad_strided = input_dot(back_side, project_a)
        grad_active_two = input_dot(back_three, expand_a)
        grad_conv_two, gain_two, bias_two = norm_backward(
            grad_active_two * silu_slope(normed_two),
            mask_coarse,
            count_coarse,
            spatial_gain_a,
            scaled_two,
            inverse_two,
            pixel_total,
        )
        accumulate(totals, "spatial_gain_a", gain_two)
        accumulate(totals, "spatial_bias_a", bias_two)
        rounded_two = grad_conv_two.astype(jnp.bfloat16)
        wide_spatial_a = weight_dot(patches_one, rounded_two)
        grad_extended_one = spread_taps(
            input_dot(rounded_two, spatial_a), extended_one, 2, coarse_rows, half_side
        )
        below_row = passed_along(grad_extended_one[:1].astype(jnp.bfloat16), "rows", -1).astype(
            jnp.float32
        )
        grad_active_one = grad_extended_one[1:].at[-1].add(below_row[0])
        grad_conv_one, gain_one, bias_one = norm_backward(
            grad_active_one * silu_slope(normed_one),
            mask_fine,
            count_fine,
            reduce_gain_a,
            scaled_one,
            inverse_one,
            pixel_total,
        )
        accumulate(totals, "reduce_gain_a", gain_one)
        accumulate(totals, "reduce_bias_a", bias_one)
        rounded_one = grad_conv_one.astype(jnp.bfloat16)
        wide_reduce_a = weight_dot(source, rounded_one)
        grad_source = input_dot(rounded_one, reduce_a)
        grad_source = grad_source.at[::2, :, ::2, :].add(grad_strided)
        input_grads.append(grad_source)
        early_sums = add_terms(
            early_sums,
            (
                wide_reduce_a.reshape(-1),
                wide_spatial_a.reshape(-1),
                wide_expand_a.reshape(-1),
                wide_project_a.reshape(-1),
            ),
        )
    grad_reduce_a, grad_spatial_a, grad_expand_a, grad_project_a, grad_spatial_b, grad_expand_b = (
        lax.psum_scatter(early_sums[0], ("batch", "rows"), scatter_dimension=0, tiled=True),
        lax.psum_scatter(early_sums[1], ("batch", "rows"), scatter_dimension=0, tiled=True),
        lax.psum_scatter(early_sums[2], ("batch", "rows"), scatter_dimension=0, tiled=True),
        lax.psum_scatter(early_sums[3], ("batch", "rows"), scatter_dimension=0, tiled=True),
        lax.psum_scatter(late_sums[0], ("batch", "rows"), scatter_dimension=0, tiled=True),
        lax.psum_scatter(late_sums[1], ("batch", "rows"), scatter_dimension=0, tiled=True),
    )
    narrow_weights = jnp.concatenate(
        [
            totals["reduce_b"].reshape(-1),
            totals["squeeze_a"].reshape(-1),
            totals["excite_a"].reshape(-1),
            totals["squeeze_b"].reshape(-1),
            totals["excite_b"].reshape(-1),
        ]
    )
    narrow_biases = jnp.concatenate(
        [
            totals["squeeze_bias_a"],
            totals["excite_bias_a"],
            totals["squeeze_bias_b"],
            totals["excite_bias_b"],
        ]
    )
    narrow_weights, narrow_biases = channel_total(narrow_weights, narrow_biases)
    grad_reduce_b, grad_squeeze_a, grad_excite_a, grad_squeeze_b, grad_excite_b = unpack(
        narrow_weights,
        (reduce_b.shape, squeeze_a.shape, excite_a.shape, squeeze_b.shape, excite_b.shape),
    )
    grad_squeeze_bias_a, grad_excite_bias_a, grad_squeeze_bias_b, grad_excite_bias_b = unpack(
        narrow_biases,
        (squeeze_bias_a.shape, excite_bias_a.shape, squeeze_bias_b.shape, excite_bias_b.shape),
    )
    return (
        jnp.stack(outputs),
        jnp.stack(input_grads),
        grad_reduce_a,
        totals["reduce_gain_a"],
        totals["reduce_bias_a"],
        grad_spatial_a,
        totals["spatial_gain_a"],
        totals["spatial_bias_a"],
        grad_expand_a,
        totals["expand_gain_a"],
        totals["expand_bias_a"],
        grad_project_a,
        totals["project_gain_a"],
        totals["project_bias_a"],
        grad_squeeze_a,
        grad_squeeze_bias_a,
        grad_excite_a,
        grad_excite_bias_a,
        grad_reduce_b,
        totals["reduce_gain_b"],
        totals["reduce_bias_b"],
        grad_spatial_b,
        totals["spatial_gain_b"],
        totals["spatial_bias_b"],
        grad_expand_b,
        totals["expand_gain_b"],
        totals["expand_bias_b"],
        grad_squeeze_b,
        grad_squeeze_bias_b,
        grad_excite_b,
        grad_excite_bias_b,
    )


def solution(mesh):
    in_specs = (
        P(None, "rows", "batch", None, None),
        P(),
        P(),
        P(),
        P(),
        P(),
        P(),
        P(),
        P(),
        P("rows"),
        P("rows"),
        P(),
        P("rows"),
        P("rows"),
        P("rows", None),
        P(),
        P(None, "rows"),
        P("rows"),
        P("rows", None),
        P(),
        P(),
        P(),
        P(),
        P(),
        P(),
        P("rows"),
        P("rows"),
        P("rows", None),
        P(),
        P(None, "rows"),
        P("rows"),
        P(None, None, "batch", None, "rows"),
    )
    out_specs = (
        P(None, None, "batch", None, "rows"),
        P(None, "rows", "batch", None, None),
        P(("batch", "rows")),
        P(),
        P(),
        P(("batch", "rows")),
        P(),
        P(),
        P(("batch", "rows")),
        P("rows"),
        P("rows"),
        P(("batch", "rows")),
        P("rows"),
        P("rows"),
        P("rows", None),
        P(),
        P(None, "rows"),
        P("rows"),
        P("rows", None),
        P(),
        P(),
        P(("batch", "rows")),
        P(),
        P(),
        P(("batch", "rows")),
        P("rows"),
        P("rows"),
        P("rows", None),
        P(),
        P(None, "rows"),
        P("rows"),
    )
    return jax.shard_map(
        per_device, mesh=mesh, in_specs=in_specs, out_specs=out_specs, check_vma=False
    )
```

profile of v0, /device:TPU:0, one launch (start us, length us, event | category | flops | bytes accessed | tf_op | source)
XLA Modules:
  0.0 2196.6 jit_solution(5001951781179235365)
XLA Ops:
  23.5 12.0 reshape.1212
  47.6 42.1 %all-reduce.53 = (f32[512]{0:T(512)S(1)}, f32[512]{0:T(512)S(1)}, f32[512]{0:T(512)S(1)}, f32[512]{0:T(512)S(1)}) all-reduce(f32[512]{0:T(512)S(1)} %get-tuple-element.225, f32[512]{0:T(512)S(1)} %get-tuple-element.224, f32[512]{0:T(512)S(1)} %get-tuple-element.217, ...), channel_id=1, replica_groups=mesh['batch'=16,'rows'=2] {'batch','rows'}, use_global_device_ids=true, to_apply=%region_39.40 | all-reduce | flops 2048 | bytes 16384 | tf_op jit(solution)/shard_map/psum | solution.py:89
  114.2 12.0 reshape.1206
  130.3 12.8 reshape.1213
  143.1 12.7 copy.114
  157.2 12.0 reshape.1207
  169.2 12.7 copy.120
  216.8 40.3 %all-reduce.52 = (f32[512]{0:T(512)S(1)}, f32[512]{0:T(512)S(1)}, f32[512]{0:T(512)S(1)}, f32[512]{0:T(512)S(1)}) all-reduce(f32[512]{0:T(512)S(1)} %get-tuple-element.237, f32[512]{0:T(512)S(1)} %get-tuple-element.236, f32[512]{0:T(512)S(1)} %get-tuple-element.233, ...), channel_id=1, replica_groups=mesh['batch'=16,'rows'=2] {'batch','rows'}, use_global_device_ids=true, to_apply=%region_44.45 | all-reduce | flops 2048 | bytes 16384 | tf_op jit(solution)/shard_map/psum | solution.py:89
  285.6 12.0 reshape.1215
  324.2 12.0 reshape.1208
  342.5 12.8 reshape.1209
  355.4 12.7 copy.118
  369.8 76.6 %all-reduce.59 = (f32[1024]{0:T(1024)S(1)}, f32[1024]{0:T(1024)S(1)}, f32[1024]{0:T(1024)S(1)}, f32[1024]{0:T(1024)S(1)}) all-reduce(f32[1024]{0:T(1024)S(1)} %get-tuple-element.221, f32[1024]{0:T(1024)S(1)} %get-tuple-element.220, f32[1024]{0:T(1024)S(1)} %get-tuple-element.213, ...), channel_id=1, replica_groups=mesh['batch'=16,'rows'=2] {'batch'}, use_global_device_ids=true, to_apply=%region_46.47 | all-reduce | flops 4096 | bytes 32768 | tf_op jit(solution)/shard_map/psum | solution.py:93
  450.5 71.8 %all-reduce.58 = (f32[1024]{0:T(1024)}, f32[1024]{0:T(1024)S(1)}, f32[1024]{0:T(1024)}, f32[1024]{0:T(1024)S(1)}) all-reduce(f32[1024]{0:T(1024)} %get-tuple-element.449, f32[1024]{0:T(1024)} %get-tuple-element.450, f32[1024]{0:T(1024)S(1)} %get-tuple-element.215, ...), channel_id=1, replica_groups=mesh['batch'=16,'rows'=2] {'batch'}, use_global_device_ids=true, to_apply=%region_52.53 | all-reduce | flops 4096 | bytes 32768 | tf_op jit(solution)/shard_map/psum | solution.py:93
  554.0 40.6 %all-reduce.51 = (f32[512]{0:T(512)S(1)}, f32[512]{0:T(512)S(1)}, f32[512]{0:T(512)S(1)}, f32[512]{0:T(512)S(1)}) all-reduce(f32[512]{0:T(512)S(1)} %get-tuple-element.253, f32[512]{0:T(512)S(1)} %get-tuple-element.252, f32[512]{0:T(512)S(1)} %get-tuple-element.251, ...), channel_id=1, replica_groups=mesh['batch'=16,'rows'=2] {'batch','rows'}, use_global_device_ids=true, to_apply=%region_59.60 | all-reduce | flops 2048 | bytes 16384 | tf_op jit(solution)/shard_map/psum | solution.py:89
  612.4 40.1 %all-reduce.50 = (f32[512]{0:T(512)S(1)}, f32[512]{0:T(512)S(1)}, f32[512]{0:T(512)S(1)}, f32[512]{0:T(512)S(1)}) all-reduce(f32[512]{0:T(512)S(1)} %get-tuple-element.235, f32[512]{0:T(512)S(1)} %get-tuple-element.234, f32[512]{0:T(512)S(1)} %get-tuple-element.231, ...), channel_id=1, replica_groups=mesh['batch'=16,'rows'=2] {'batch','rows'}, use_global_device_ids=true, to_apply=%region_63.64 | all-reduce | flops 2048 | bytes 16384 | tf_op jit(solution)/shard_map/psum | solution.py:89
  654.4 11.7 copy.121
  666.2 12.0 reshape.1210
  684.4 12.8 reshape.1211
  697.2 12.8 copy.122
  723.0 12.0 reshape.1216
  741.3 12.8 reshape.1217
  754.1 12.7 copy.116
  768.6 76.6 %all-reduce.57 = (f32[1024]{0:T(1024)S(1)}, f32[1024]{0:T(1024)S(1)}, f32[1024]{0:T(1024)S(1)}, f32[1024]{0:T(1024)S(1)}) all-reduce(f32[1024]{0:T(1024)S(1)} %get-tuple-element.211, f32[1024]{0:T(1024)S(1)} %get-tuple-element.210, f32[1024]{0:T(1024)S(1)} %get-tuple-element.219, ...), channel_id=1, replica_groups=mesh['batch'=16,'rows'=2] {'batch'}, use_global_device_ids=true, to_apply=%region_30.31 | all-reduce | flops 4096 | bytes 32768 | tf_op jit(solution)/shard_map/psum | solution.py:93
  869.4 71.8 %all-reduce.56 = (f32[1024]{0:T(1024)S(1)}, f32[1024]{0:T(1024)S(1)}, f32[1024]{0:T(1024)S(1)}, f32[1024]{0:T(1024)S(1)}) all-reduce(f32[1024]{0:T(1024)S(1)} %get-tuple-element.203, f32[1024]{0:T(1024)S(1)} %get-tuple-element.202, f32[1024]{0:T(1024)S(1)} %get-tuple-element.199, ...), channel_id=1, replica_groups=mesh['batch'=16,'rows'=2] {'batch'}, use_global_device_ids=true, to_apply=%region_108.109 | all-reduce | flops 4096 | bytes 32768 | tf_op jit(solution)/shard_map/psum | solution.py:93
  956.2 37.3 %all-reduce.49 = (f32[512]{0:T(512)S(1)}, f32[512]{0:T(512)S(1)}, f32[512]{0:T(512)S(1)}, f32[512]{0:T(512)S(1)}) all-reduce(f32[512]{0:T(512)S(1)} %get-tuple-element.249, f32[512]{0:T(512)S(1)} %get-tuple-element.248, f32[512]{0:T(512)S(1)} %copy-done.336, ...), channel_id=1, replica_groups=mesh['batch'=16,'rows'=2] {'batch','rows'}, use_global_device_ids=true, to_apply=%region_112.113 | all-reduce | flops 2048 | bytes 16384 | tf_op jit(solution)/shard_map/psum | solution.py:89
  1050.3 41.1 %all-reduce.48 = (f32[512]{0:T(512)S(1)}, f32[512]{0:T(512)S(1)}, f32[512]{0:T(512)S(1)}, f32[512]{0:T(512)S(1)}) all-reduce(f32[512]{0:T(512)S(1)} %get-tuple-element.454, f32[512]{0:T(512)S(1)} %get-tuple-element.455, f32[512]{0:T(512)S(1)} %get-tuple-element.241, ...), channel_id=1, replica_groups=mesh['batch'=16,'rows'=2] {'batch','rows'}, use_global_device_ids=true, to_apply=%region_116.117 | all-reduce | flops 2048 | bytes 16384 | tf_op jit(solution)/shard_map/psum | solution.py:89
  1109.7 76.3 %all-reduce.55 = (f32[1024]{0:T(1024)S(1)}, f32[1024]{0:T(1024)S(1)}, f32[1024]{0:T(1024)S(1)}, f32[1024]{0:T(1024)S(1)}, f32[1024]{0:T(1024)S(1)}, /*index=5*/f...) all-reduce(f32[1024]{0:T(1024)S(1)} %get-tuple-element.201, ...), channel_id=1, replica_groups=mesh['batch'=16,'rows'=2] {'batch'}, use_global_device_ids=true, to_apply=%region_122.123 | all-reduce | flops 10496 | bytes 83968 | tf_op jit(solution)/shard_map/psum | solution.py:93
  1202.1 36.9 %all-reduce.47 = (f32[512]{0:T(512)S(1)}, f32[512]{0:T(512)S(1)}, f32[512]{0:T(512)S(1)}, f32[512]{0:T(512)S(1)}) all-reduce(f32[512]{0:T(512)S(1)} %get-tuple-element.245, f32[512]{0:T(512)S(1)} %get-tuple-element.244, f32[512]{0:T(512)S(1)} %get-tuple-element.239, ...), channel_id=1, replica_groups=mesh['batch'=16,'rows'=2] {'batch','rows'}, use_global_device_ids=true, to_apply=%region_126.127 | all-reduce | flops 2048 | bytes 16384 | tf_op jit(solution)/shard_map/psum | solution.py:89
  1502.6 41.5 %all-reduce.46 = (f32[512]{0:T(512)S(1)}, f32[512]{0:T(512)S(1)}, f32[512]{0:T(512)S(1)}, f32[512]{0:T(512)S(1)}) all-reduce(f32[512]{0:T(512)S(1)} %get-tuple-element.451, f32[512]{0:T(512)S(1)} %get-tuple-element.452, f32[512]{0:T(512)S(1)} %get-tuple-element.227, ...), channel_id=1, replica_groups=mesh['batch'=16,'rows'=2] {'batch','rows'}, use_global_device_ids=true, to_apply=%region_130.131 | all-reduce | flops 2048 | bytes 16384 | tf_op jit(solution)/shard_map/psum | solution.py:89
  1599.7 16.6 all-reduce.67.cloned.1.call-done
  1626.8 553.4 %all-reduce.69.cloned.1.call-done = (f32[524288]{0:T(1024)}, f32[2359296]{0:T(1024)}, f32[1048576]{0:T(1024)}, f32[2097152]{0:T(1024)}, f32[2359296]{0:T(1024)}, /*index=5*/f32[1048576]{0:T(1024)}) async-done(((f32[524288]{0:T(1024)}, f32[2359296]{0:T(1024)}, f32[1048576]{0:T(1024)}, f32[2097152]{0:T(1024)}, f32[2359296]{0:T(1024)}, /*index=5*/f32[1048576]{0:T(1024)}), (f32[524288]{0:T(1024)}, ...) | async-done | bytes 37748752
  (1105 shorter events, 701.3 us)
Async XLA Ops:
  7.2 645.9 %copy-start = (bf16[512,2048]{1,0:T(8,128)(2,1)S(1)}, bf16[512,2048]{1,0:T(8,128)(2,1)}, u32[]{:S(2)}) copy-start(bf16[512,2048]{1,0:T(8,128)(2,1)} %param.68) | copy-start | bytes 6291460
  35.5 90.7 %all-to-all-start.1 = ((bf16[2,2,65536]{2,1,0:T(2,128)(2,1)}), bf16[2,2,65536]{2,1,0:T(2,128)(2,1)}, u32[]{:S(2)}, u32[]{:S(2)}) async-start(bf16[2,2,65536]{2,1,0:T(2,128)(2,1)} %reshape.1212), calls=%async_computation.1 | async-start | bytes 1048576 | tf_op jit(solution)/shard_map/all_to_all | solution.py:247
  92.4 89.5 %collective-permute-start = (bf16[1,4,16,512]{3,2,1,0:T(8,128)(2,1)S(1)}, bf16[1,4,16,512]{3,2,1,0:T(8,128)(2,1)}, u32[]{:S(2)}, u32[]{:S(2)}) collective-permute-start(bf16[1,4,16,512]{3,2,1,0:T(8,128)(2,1)S(1)} %slice.551), channel_id=1, source_target_pairs={{0,1},{2,3},{4,5},{6,7},{8,9},{10,11},{12,13},{14,15},{16,17},{18,... | collective-permute-start | bytes 196616 | tf_op jit(solution)/shard_map/ppermute | solution.py:15
  94.9 100.7 %collective-permute-start.3 = (bf16[1,4,16,512]{3,2,1,0:T(8,128)(2,1)}, bf16[1,4,16,512]{3,2,1,0:T(8,128)(2,1)}, u32[]{:S(2)}, u32[]{:S(2)}) collective-permute-start(bf16[1,4,16,512]{3,2,1,0:T(8,128)(2,1)} %slice.560), channel_id=1, source_target_pairs={{0,1},{2,3},{4,5},{6,7},{8,9},{10,11},{12,13},{14,15},{16,17},{18,... | collective-permute-start | bytes 196616 | tf_op jit(solution)/shard_map/ppermute | solution.py:15
  97.5 211.7 %copy-start.100 = (f32[4,4,8]{2,1,0:T(4,128)}, f32[4,4,8]{2,1,0:T(4,128)S(1)}, u32[]{:S(2)}) copy-start(f32[4,4,8]{2,1,0:T(4,128)S(1)} %and_convert_fusion.6) | copy-start | bytes 1540
  104.0 1082.0 %copy-start.72 = (f32[8,4,8]{2,1,0:T(4,128)}, f32[8,4,8]{2,1,0:T(4,128)S(1)}, u32[]{:S(2)}) copy-start(f32[8,4,8]{2,1,0:T(4,128)S(1)} %and_convert_fusion.3) | copy-start | bytes 3076
  104.1 845.6 %copy-start.74 = (f32[8,4,8]{2,1,0:T(4,128)}, f32[8,4,8]{2,1,0:T(4,128)S(1)}, u32[]{:S(2)}) copy-start(f32[8,4,8]{2,1,0:T(4,128)S(1)} %and_convert_fusion) | copy-start | bytes 3076
  104.2 153.5 %copy-start.104 = (f32[4,4,8]{2,1,0:T(4,128)}, f32[4,4,8]{2,1,0:T(4,128)S(1)}, u32[]{:S(2)}) copy-start(f32[4,4,8]{2,1,0:T(4,128)S(1)} %and_convert_fusion.7) | copy-start | bytes 1540
  126.2 30.9 %all-to-all-start.4 = ((bf16[2,2,65536]{2,1,0:T(2,128)(2,1)}), bf16[2,2,65536]{2,1,0:T(2,128)(2,1)S(1)}, u32[]{:S(2)}, u32[]{:S(2)}) async-start(bf16[2,2,65536]{2,1,0:T(2,128)(2,1)} %reshape.1206), calls=%async_computation.5 | async-start | bytes 1048576 | tf_op jit(solution)/shard_map/all_to_all | solution.py:247
  129.7 411.9 %reduce-scatter.5.cloned.1.call-start = ((), (), s32[]{:S(2)}) async-start(), calls=%async_computation.15 | async-start | bytes 393216 | tf_op jit(solution)/shard_map/reduce_scatter | solution.py:270
  309.2 876.9 %copy-start.2 = (f32[4,4,8,2,1024]{4,2,1,0,3:T(8,128)}, f32[4,4,8,2,1024]{4,2,1,0,3:T(8,128)S(1)}, u32[]{:S(2)}) copy-start(f32[4,4,8,2,1024]{4,2,1,0,3:T(8,128)S(1)} %copy.112) | copy-start | bytes 3145732
  537.5 15.5 reduce-scatter.3.cloned.1.call-start
  541.6 1074.7 %all-reduce.67.cloned.1.call-start = ((), (), s32[]{:S(2)}) async-start(), calls=%async_computation.16 | async-start | bytes 8388608 | tf_op jit(solution)/shard_map/psum | solution.py:93
  596.5 9.2 collective-permute-start.5
  597.8 7.9 collective-permute-start.4
  600.8 5.3 collective-permute-start.2
  602.1 4.0 collective-permute-start.1
  845.9 95.3 %copy-start.142 = (f32[1024]{0:T(1024)}, f32[1024]{0:T(1024)S(1)}, u32[]{:S(2)}) copy-start(f32[1024]{0:T(1024)S(1)} %get-tuple-element.458) | copy-start | bytes 12292
  845.9 103.9 %copy-start.144 = (f32[1024]{0:T(1024)}, f32[1024]{0:T(1024)S(1)}, u32[]{:S(2)}) copy-start(f32[1024]{0:T(1024)S(1)} %get-tuple-element.380) | copy-start | bytes 12292
  845.9 103.8 %copy-start.154 = (f32[1024]{0:T(1024)}, f32[1024]{0:T(1024)S(1)}, u32[]{:S(2)}) copy-start(f32[1024]{0:T(1024)S(1)} %add_rsqrt_fusion) | copy-start | bytes 12292
  853.4 96.4 %copy-start.79 = (f32[4,1024]{1,0:T(4,128)}, f32[4,1024]{1,0:T(4,128)S(1)}, u32[]{:S(2)}) copy-start(f32[4,1024]{1,0:T(4,128)S(1)} %fusion.91) | copy-start | bytes 49156
  854.3 148.8 %copy-start.85 = (f32[4,1024]{1,0:T(4,128)}, f32[4,1024]{1,0:T(4,128)S(1)}, u32[]{:S(2)}) copy-start(f32[4,1024]{1,0:T(4,128)S(1)} %fusion.99) | copy-start | bytes 49156
  1004.6 41.1 %collective-permute-start.7 = (bf16[1,4,8,512]{3,2,1,0:T(8,128)(2,1)S(1)}, bf16[1,4,8,512]{3,2,1,0:T(8,128)(2,1)}, u32[]{:S(2)}, u32[]{:S(2)}) collective-permute-start(bf16[1,4,8,512]{3,2,1,0:T(8,128)(2,1)S(1)} %get-tuple-element.434), channel_id=1, source_target_pairs={{1,0},{3,2},{5,4},{7,6},{9,8},{11,10},{13,12},{15,14},{17,16},{19,... | collective-permute-start | bytes 98312 | tf_op jit(solution)/shard_map/ppermute | solution.py:26
  1005.9 39.8 %collective-permute-start.6 = (bf16[1,4,8,512]{3,2,1,0:T(8,128)(2,1)S(1)}, bf16[1,4,8,512]{3,2,1,0:T(8,128)(2,1)}, u32[]{:S(2)}, u32[]{:S(2)}) collective-permute-start(bf16[1,4,8,512]{3,2,1,0:T(8,128)(2,1)S(1)} %get-tuple-element.433), channel_id=1, source_target_pairs={{0,1},{2,3},{4,5},{6,7},{8,9},{10,11},{12,13},{14,15},{16,17},{18,... | collective-permute-start | bytes 98312 | tf_op jit(solution)/shard_map/ppermute | solution.py:25
  1013.5 33.9 %collective-permute-start.10 = (bf16[1,4,8,512]{3,2,1,0:T(8,128)(2,1)}, bf16[1,4,8,512]{3,2,1,0:T(8,128)(2,1)}, u32[]{:S(2)}, u32[]{:S(2)}) collective-permute-start(bf16[1,4,8,512]{3,2,1,0:T(8,128)(2,1)} %get-tuple-element.436), channel_id=1, source_target_pairs={{1,0},{3,2},{5,4},{7,6},{9,8},{11,10},{13,12},{15,14},{17,16},{19,... | collective-permute-start | bytes 98312 | tf_op jit(solution)/shard_map/ppermute | solution.py:26
  1014.8 32.6 %collective-permute-start.9 = (bf16[1,4,8,512]{3,2,1,0:T(8,128)(2,1)S(1)}, bf16[1,4,8,512]{3,2,1,0:T(8,128)(2,1)}, u32[]{:S(2)}, u32[]{:S(2)}) collective-permute-start(bf16[1,4,8,512]{3,2,1,0:T(8,128)(2,1)S(1)} %get-tuple-element.435), channel_id=1, source_target_pairs={{0,1},{2,3},{4,5},{6,7},{8,9},{10,11},{12,13},{14,15},{16,17},{18,... | collective-permute-start | bytes 98312 | tf_op jit(solution)/shard_map/ppermute | solution.py:25
  1239.0 95.8 %copy-start.299 = (f32[512]{0:T(512)}, f32[512]{0:T(512)S(1)}, u32[]{:S(2)}) copy-start(f32[512]{0:T(512)S(1)} %get-tuple-element.269) | copy-start | bytes 6148
  1239.0 95.8 %copy-start.303 = (f32[512]{0:T(512)}, f32[512]{0:T(512)S(1)}, u32[]{:S(2)}) copy-start(f32[512]{0:T(512)S(1)} %get-tuple-element.268) | copy-start | bytes 6148
  1333.3 161.8 %collective-permute-start.8 = (bf16[1,4,16,512]{3,2,1,0:T(8,128)(2,1)}, bf16[1,4,16,512]{3,2,1,0:T(8,128)(2,1)S(1)}, u32[]{:S(2)}, u32[]{:S(2)}) collective-permute-start(bf16[1,4,16,512]{3,2,1,0:T(8,128)(2,1)} %slice.637), channel_id=1, source_target_pairs={{1,0},{3,2},{5,4},{7,6},{9,8},{11,10},{13,12},{15,14},{17,16},{19,... | collective-permute-start | bytes 196616 | tf_op jit(solution)/shard_map/ppermute | solution.py:15
  1413.4 82.7 %collective-permute-start.11 = (bf16[1,4,16,512]{3,2,1,0:T(8,128)(2,1)}, bf16[1,4,16,512]{3,2,1,0:T(8,128)(2,1)}, u32[]{:S(2)}, u32[]{:S(2)}) collective-permute-start(bf16[1,4,16,512]{3,2,1,0:T(8,128)(2,1)} %slice.636), channel_id=1, source_target_pairs={{1,0},{3,2},{5,4},{7,6},{9,8},{11,10},{13,12},{15,14},{17,16},{19,... | collective-permute-start | bytes 196616 | tf_op jit(solution)/shard_map/ppermute | solution.py:15
  1447.4 732.9 %all-reduce.69.cloned.1.call-start = ((), (), s32[]{:S(2)}) async-start(), calls=%async_computation.17 | async-start | bytes 75497472
  1623.1 566.9 %copy-start.1 = (bf16[512,2048]{1,0:T(8,128)(2,1)S(1)}, bf16[512,2048]{1,0:T(8,128)(2,1)}, u32[]{:S(2)}) copy-start(bf16[512,2048]{1,0:T(8,128)(2,1)} %param.68) | copy-start | bytes 6291460
  (349 other events, 4199.4 us)
Sparse Core Ops, SparseCore 0:
  537.6 3.5 reduce-scatter.4
  544.1 8.8 reduce-scatter.2
  1447.5 168.8 all-reduce.66
  1623.8 556.4 all-reduce.68
where the time goes:
time: 2220 us; the launch traced here: 2200 us
  blocking collectives  758 us (34%)
  waiting for transfers between devices  580 us (26%)
  local copies, waits for them, and re-layouts  563 us (25%)
  matrix products  134 us (6%)
  other arithmetic  105 us (5%)
  starting transfers between devices  35.8 us (2%)
    unnamed x5, waiting for transfers between devices  554 us
    psum x5, blocking collectives, channel_total(): return lax.psum((first, second), 'batch')  373 us
    psum x8, blocking collectives, pixel_total(): return lax.psum((first, second), ('batch', 'rows'))  320 us
    unnamed x784, local copies, waits for them, and re-layouts  224 us
    pad x18, local copies, waits for them, and re-layouts, gather_taps(): padded[row_tap:row_tap + stride * out_rows:stride, :, col_tap:col_tap + s...  136 us
    dot_general x14, matrix products, weight_dot(): lax.dot_general(inputs, grads, ((leading, leading), ((), ())), preferred_...  47.7 us
  transfers between devices with their start and end apart: 18, of which 3 were waited for; matrix products, arithmetic and copies ran while one was open for 16% of the time, Pallas kernels for 0%

commit v1 on v0

v1 whole, which is shorter than its diff:
```python
import jax
import jax.numpy as jnp
from jax import lax
from jax.sharding import PartitionSpec as P

epsilon = 1e-05
HIGHEST = lax.Precision.HIGHEST
BF16 = jnp.bfloat16
F32 = jnp.float32

PLANE_TAPS = (((1, 0),), ((2, 0), (0, 1)))


def swapped(block, axis, mask):
    route = [(i, i ^ mask) for i in range(lax.axis_size(axis))]
    return lax.ppermute(block, axis, route)


def bits_of(size):
    return [1 << k for k in range(size.bit_length() - 1)]


def all_sum(parts):
    parts = parts + swapped(parts, "rows", 1)
    size = lax.axis_size("batch")
    spread = jnp.broadcast_to(parts[None], (size,) + parts.shape)
    return jnp.sum(lax.all_to_all(spread, "batch", 0, 0, tiled=True), axis=0)


def halved(block, orders):
    size = lax.axis_size("batch")
    place = lax.axis_index("batch")
    bits = bits_of(size)
    count = block.shape[1]
    cut = count // 2 // 16 * 16
    parts = []
    for part, order in zip((block[:, :cut], block[:, cut:]), orders(bits)):
        shape = part.shape[1:]
        left = list(reversed(bits))
        part = part.reshape((2,) * len(bits) + shape)
        for bit in order:
            axis = left.index(bit)
            mine = (place // bit) % 2
            gone = lax.dynamic_index_in_dim(part, 1 - mine, axis, keepdims=False)
            kept = lax.dynamic_index_in_dim(part, mine, axis, keepdims=False)
            total = kept.astype(F32) + swapped(gone, "batch", bit).astype(F32)
            left.pop(axis)
            part = total.astype(BF16) if left else total
        parts.append(part)
    return jnp.concatenate(parts, axis=0)


def two_orders(bits):
    return (bits, bits[1::-1] + bits[2:])


def collected(block):
    place = lax.axis_index("batch")
    block = block[None]
    for bit in bits_of(lax.axis_size("batch")):
        other = swapped(block, "batch", bit)
        upper = (place // bit) % 2 == 1
        block = jnp.concatenate([jnp.where(upper, other, block), jnp.where(upper, block, other)], axis=0)
    return block


def core_sum(block, axis):
    core = lax.axis_index("rows")
    gone = lax.dynamic_index_in_dim(block, 1 - core, axis, keepdims=False)
    kept = lax.dynamic_index_in_dim(block, core, axis, keepdims=False)
    return (kept.astype(F32) + swapped(gone, "rows", 1).astype(F32)).astype(BF16)


def both_cores(block, axis):
    core = lax.axis_index("rows")
    other = swapped(block, "rows", 1)
    first = jnp.where(core == 0, block, other)
    second = jnp.where(core == 0, other, block)
    return jnp.concatenate([first, second], axis=axis)


def silu_slope(values):
    sigma = jax.nn.sigmoid(values)
    return sigma * (1.0 + values * (1.0 - sigma))


def forward_dot(inputs, weight):
    return jnp.dot(inputs, weight, preferred_element_type=F32)


def input_dot(grads, weight):
    return lax.dot_general(
        grads, weight, (((grads.ndim - 1,), (1,)), ((), ())), preferred_element_type=F32
    )


def weight_dot(inputs, grads):
    leading = tuple(range(inputs.ndim - 1))
    return lax.dot_general(
        inputs, grads, ((leading, leading), ((), ())), preferred_element_type=F32
    )


def shifted(values, rows, cols):
    zero = jnp.zeros((), values.dtype)
    pads = [(0, 0, 0)] * values.ndim
    pads[1] = (-rows, rows, 0)
    pads[3] = (-cols, cols, 0)
    if rows == 0 and cols == 0:
        return values
    return lax.pad(values, zero, pads)


PIX = (1, 2, 3)
FPIX = (0, 1, 3, 4, 5)


def moments(first, second, axes):
    return jnp.stack([jnp.sum(first, axis=axes), jnp.sum(first * second, axis=axes)], axis=1)


def wide(vector):
    return vector[:, None, None, None, :]


def norm_of(sums, counted):
    centre = sums[:, 0] / counted
    inverse = lax.rsqrt(sums[:, 1] / counted - centre * centre + epsilon)
    return wide(centre), wide(inverse)


def norm_back(live_grad, scaled, inverse, gain, sums, counted, inside):
    mean = wide(sums[:, 0] / counted)
    slope = wide(sums[:, 1] / counted)
    return ((live_grad - (mean + scaled * slope)) * (gain * inverse) * inside).astype(BF16)


def gate_forward(normed, pixel_count, squeeze, squeeze_bias, excite, excite_bias):
    pooled = jnp.sum(normed, axis=(1, 3)) / pixel_count[..., None]
    pooled = pooled.reshape(-1, pooled.shape[-1])
    inner = jnp.dot(pooled, squeeze.astype(F32), precision=HIGHEST) + squeeze_bias
    hidden = jax.nn.silu(inner)
    gating = jax.nn.sigmoid(jnp.dot(hidden, excite.astype(F32), precision=HIGHEST) + excite_bias)
    return gating, (pooled, inner, hidden)


def gate_backward(gate_grad, gating, cache, pixel_count, squeeze, excite):
    pooled, inner, hidden = cache
    logit_grad = gate_grad * gating * (1.0 - gating)
    excite_grad = jnp.dot(hidden.T, logit_grad, precision=HIGHEST)
    hidden_grad = jnp.dot(logit_grad, excite.astype(F32).T, precision=HIGHEST)
    inner_grad = hidden_grad * silu_slope(inner)
    squeeze_grad = jnp.dot(pooled.T, inner_grad, precision=HIGHEST)
    pooled_grad = jnp.dot(inner_grad, squeeze.astype(F32).T, precision=HIGHEST)
    biases = (jnp.sum(inner_grad, axis=0), jnp.sum(logit_grad, axis=0))
    return pooled_grad / pixel_count.reshape(-1, 1), squeeze_grad, excite_grad, biases


def per_map(values, micro, images):
    return values.reshape(micro, 1, images, 1, values.shape[-1])


def folded(grad):
    size = lax.axis_size("batch")
    rows, width = grad.shape
    grad = grad.astype(BF16).reshape(size, 2, rows // (2 * size), width // 512, 512)
    return jnp.swapaxes(grad, 2, 3).reshape(size, 2, -1, 512)


def unfolded(block, width):
    count = width // 512
    rows = block.shape[0] // count
    return jnp.swapaxes(block.reshape(count, rows, 512), 0, 1).reshape(-1)


def per_device(
    images,
    crop_sizes,
    reduce_a,
    reduce_gain_a,
    reduce_bias_a,
    spatial_a,
    spatial_gain_a,
    spatial_bias_a,
    expand_a,
    expand_gain_a,
    expand_bias_a,
    project_a,
    project_gain_a,
    project_bias_a,
    squeeze_a,
    squeeze_bias_a,
    excite_a,
    excite_bias_a,
    reduce_b,
    reduce_gain_b,
    reduce_bias_b,
    spatial_b,
    spatial_gain_b,
    spatial_bias_b,
    expand_b,
    expand_gain_b,
    expand_bias_b,
    squeeze_b,
    squeeze_bias_b,
    excite_b,
    excite_bias_b,
    cotangent,
):
    micro = images.shape[0]
    held = images.shape[2] // 2
    side = images.shape[3]
    half = side // 2
    core = lax.axis_index("rows")
    batch_index = lax.axis_index("batch")

    mine = lax.dynamic_slice_in_dim(images, core * held, held, axis=2)
    away = lax.dynamic_slice_in_dim(images, (1 - core) * held, held, axis=2)
    other = swapped(away, "rows", 1)
    source = jnp.concatenate(
        [jnp.where(core == 0, mine, other), jnp.where(core == 0, other, mine)], axis=1
    )
    mine = lax.dynamic_slice_in_dim(cotangent, core * held, held, axis=2)
    away = lax.dynamic_slice_in_dim(cotangent, (1 - core) * held, held, axis=2)
    other = swapped(away, "rows", 1)
    upstream = jnp.concatenate(
        [jnp.where(core == 0, mine, other), jnp.where(core == 0, other, mine)], axis=4
    )
    vectors = jnp.stack(
        [
            expand_gain_a,
            expand_bias_a,
            project_gain_a,
            project_bias_a,
            excite_bias_a,
            expand_gain_b,
            expand_bias_b,
            excite_bias_b,
        ]
    )
    vectors = both_cores(vectors, 1)
    tall = both_cores(jnp.concatenate([reduce_b, squeeze_a, squeeze_b], axis=1), 0)
    flat = both_cores(jnp.concatenate([excite_a, excite_b], axis=0), 1)
    expand_gain_a, expand_bias_a, project_gain_a, project_bias_a = (vectors[k] for k in range(4))
    excite_bias_a, expand_gain_b, expand_bias_b, excite_bias_b = (vectors[k] for k in range(4, 8))
    mid = reduce_b.shape[1]
    hid = squeeze_a.shape[1]
    reduce_b, squeeze_a, squeeze_b = tall[:, :mid], tall[:, mid : mid + hid], tall[:, mid + hid :]
    excite_a, excite_b = flat[:hid], flat[hid:]

    half_all = crop_sizes // 2
    count_fine = jnp.sum(crop_sizes * crop_sizes, axis=1).astype(F32)[:, None]
    count_coarse = jnp.sum(half_all * half_all, axis=1).astype(F32)[:, None]
    start = batch_index * 2 * held + core * held
    crops = lax.dynamic_slice_in_dim(crop_sizes, start, held, axis=1)
    halves = crops // 2
    pixel_count = (halves * halves).astype(F32)
    spots = jnp.arange(half, dtype=jnp.int32)

    def mask_of(limits, rows, cols):
        limits = limits[:, None, :, None]
        inside = (rows[None, :, None, None] < limits) & (cols[None, None, None, :] < limits)
        return inside.astype(F32)[..., None]

    mask_coarse = mask_of(halves, spots, spots)
    mask_fine = jnp.stack(
        [
            jnp.stack([mask_of(crops, 2 * spots + pr, 2 * spots + pc) for pc in range(2)])
            for pr in range(2)
        ]
    )

    planes = source.reshape(micro, half, 2, held, half, 2, source.shape[-1])
    planes = planes.transpose(2, 5, 0, 1, 3, 4, 6)

    conv_one = forward_dot(planes, reduce_a)
    strided = planes[0, 0]
    projected = forward_dot(strided, project_a).astype(BF16).astype(F32)
    sums_one = all_sum(moments(conv_one * mask_fine, conv_one, FPIX))
    centre_one, inverse_one = norm_of(sums_one, count_fine)
    scaled_one = (conv_one - centre_one) * inverse_one
    normed_one = (scaled_one * reduce_gain_a + reduce_bias_a) * mask_fine
    active_one = jax.nn.silu(normed_one).astype(BF16)
    taps = ((1, -1), (0, 0), (1, 0))
    patches_one = jnp.concatenate(
        [
            shifted(active_one[taps[i][0], taps[j][0]], taps[i][1], taps[j][1])
            for i in range(3)
            for j in range(3)
        ],
        axis=4,
    )
    conv_two = forward_dot(patches_one, spatial_a)
    sums_two = all_sum(moments(conv_two * mask_coarse, conv_two, PIX))
    centre_two, inverse_two = norm_of(sums_two, count_coarse)
    scaled_two = (conv_two - centre_two) * inverse_two
    normed_two = (scaled_two * spatial_gain_a + spatial_bias_a) * mask_coarse
    active_two = jax.nn.silu(normed_two).astype(BF16)
    expanded = forward_dot(active_two, expand_a).astype(BF16).astype(F32)
    sums_three = all_sum(
        jnp.stack(
            [
                moments(expanded * mask_coarse, expanded, PIX),
                moments(projected * mask_coarse, projected, PIX),
            ]
        )
    )
    centre_three, inverse_three = norm_of(sums_three[0], count_coarse)
    centre_side, inverse_side = norm_of(sums_three[1], count_coarse)
    scaled_three = (expanded - centre_three) * inverse_three
    scaled_side = (projected - centre_side) * inverse_side
    normed_three = (scaled_three * expand_gain_a + expand_bias_a) * mask_coarse
    normed_side = (scaled_side * project_gain_a + project_bias_a) * mask_coarse
    gate_one, cache_one = gate_forward(
        normed_three, pixel_count, squeeze_a, squeeze_bias_a, excite_a, excite_bias_a
    )
    wide_gate_one = per_map(gate_one, micro, held)
    summed_one = normed_three * wide_gate_one + normed_side
    middle = jax.nn.silu(summed_one).astype(BF16)

    conv_four = forward_dot(middle, reduce_b)
    sums_four = all_sum(moments(conv_four * mask_coarse, conv_four, PIX))
    centre_four, inverse_four = norm_of(sums_four, count_coarse)
    scaled_four = (conv_four - centre_four) * inverse_four
    normed_four = (scaled_four * reduce_gain_b + reduce_bias_b) * mask_coarse
    active_four = jax.nn.silu(normed_four).astype(BF16)
    patches_four = jnp.concatenate(
        [shifted(active_four, i - 1, j - 1) for i in range(3) for j in range(3)], axis=4
    )
    conv_five = forward_dot(patches_four, spatial_b)
    sums_five = all_sum(moments(conv_five * mask_coarse, conv_five, PIX))
    centre_five, inverse_five = norm_of(sums_five, count_coarse)
    scaled_five = (conv_five - centre_five) * inverse_five
    normed_five = (scaled_five * spatial_gain_b + spatial_bias_b) * mask_coarse
    active_five = jax.nn.silu(normed_five).astype(BF16)
    expanded_b = forward_dot(active_five, expand_b).astype(BF16).astype(F32)
    sums_six = all_sum(moments(expanded_b * mask_coarse, expanded_b, PIX))
    centre_six, inverse_six = norm_of(sums_six, count_coarse)
    scaled_six = (expanded_b - centre_six) * inverse_six
    normed_six = (scaled_six * expand_gain_b + expand_bias_b) * mask_coarse
    gate_two, cache_two = gate_forward(
        normed_six, pixel_count, squeeze_b, squeeze_bias_b, excite_b, excite_bias_b
    )
    wide_gate_two = per_map(gate_two, micro, held)
    summed_two = normed_six * wide_gate_two + middle.astype(F32)
    block_out = jax.nn.silu(summed_two).astype(BF16)

    grad_summed_two = upstream.astype(F32) * silu_slope(summed_two)
    gate_grad_two = jnp.sum(grad_summed_two * normed_six, axis=(1, 3)).reshape(gate_two.shape)
    pooled_two, grad_squeeze_b, grad_excite_b, small_two = gate_backward(
        gate_grad_two, gate_two, cache_two, pixel_count, squeeze_b, excite_b
    )
    live_six = (grad_summed_two * wide_gate_two + per_map(pooled_two, micro, held)) * mask_coarse
    back_sums_six = all_sum(moments(live_six, scaled_six, PIX))
    grad_six = norm_back(
        live_six, scaled_six, inverse_six, expand_gain_b, back_sums_six, count_coarse, mask_coarse
    )
    grad_expand_b = weight_dot(active_five, grad_six)
    live_five = input_dot(grad_six, expand_b) * silu_slope(normed_five) * mask_coarse
    back_sums_five = all_sum(moments(live_five, scaled_five, PIX))
    grad_five = norm_back(
        live_five, scaled_five, inverse_five, spatial_gain_b, back_sums_five, count_coarse, mask_coarse
    )
    grad_spatial_b = weight_dot(patches_four, grad_five)
    kernel = spatial_b.reshape(3, 3, mid, mid)
    grad_four = sum(
        input_dot(shifted(grad_five, 1 - i, 1 - j), kernel[i, j])
        for i in range(3)
        for j in range(3)
    )
    live_four = grad_four * silu_slope(normed_four) * mask_coarse
    back_sums_four = all_sum(moments(live_four, scaled_four, PIX))
    grad_four = norm_back(
        live_four, scaled_four, inverse_four, reduce_gain_b, back_sums_four, count_coarse, mask_coarse
    )
    grad_reduce_b = weight_dot(middle, grad_four)
    grad_middle = input_dot(grad_four, reduce_b) + grad_summed_two

    grad_summed_one = grad_middle * silu_slope(summed_one)
    gate_grad_one = jnp.sum(grad_summed_one * normed_three, axis=(1, 3)).reshape(gate_one.shape)
    pooled_one, grad_squeeze_a, grad_excite_a, small_one = gate_backward(
        gate_grad_one, gate_one, cache_one, pixel_count, squeeze_a, excite_a
    )
    live_three = (grad_summed_one * wide_gate_one + per_map(pooled_one, micro, held)) * mask_coarse
    live_side = grad_summed_one * mask_coarse
    back_sums_three = all_sum(
        jnp.stack([moments(live_three, scaled_three, PIX), moments(live_side, scaled_side, PIX)])
    )
    grad_three = norm_back(
        live_three,
        scaled_three,
        inverse_three,
        expand_gain_a,
        back_sums_three[0],
        count_coarse,
        mask_coarse,
    )
    grad_side = norm_back(
        live_side,
        scaled_side,
        inverse_side,
        project_gain_a,
        back_sums_three[1],
        count_coarse,
        mask_coarse,
    )
    grad_expand_a = weight_dot(active_two, grad_three)
    grad_project_a = weight_dot(strided, grad_side)
    live_two = input_dot(grad_three, expand_a) * silu_slope(normed_two) * mask_coarse
    back_sums_two = all_sum(moments(live_two, scaled_two, PIX))
    grad_two = norm_back(
        live_two, scaled_two, inverse_two, spatial_gain_a, back_sums_two, count_coarse, mask_coarse
    )
    grad_spatial_a = weight_dot(patches_one, grad_two)
    kernel = spatial_a.reshape(3, 3, mid, mid)
    grad_one = jnp.stack(
        [
            jnp.stack(
                [
                    sum(
                        input_dot(shifted(grad_two, rows, cols), kernel[i, j])
                        for i, rows in PLANE_TAPS[pr]
                        for j, cols in PLANE_TAPS[pc]
                    )
                    for pc in range(2)
                ]
            )
            for pr in range(2)
        ]
    )
    live_one = grad_one * silu_slope(normed_one) * mask_fine
    back_sums_one = all_sum(moments(live_one, scaled_one, FPIX))
    grad_one = norm_back(
        live_one, scaled_one, inverse_one, reduce_gain_a, back_sums_one, count_fine, mask_fine
    )
    grad_reduce_a = weight_dot(planes, grad_one)
    grad_one = grad_one.transpose(2, 3, 0, 4, 5, 1, 6).reshape(micro, side, held, side, mid)
    grad_source = input_dot(grad_one, reduce_a)
    grad_source = grad_source.at[:, ::2, :, ::2].add(input_dot(grad_side, project_a))

    rows_half = side // 2
    top = lax.dynamic_slice_in_dim(grad_source, core * rows_half, rows_half, axis=1)
    gone = lax.dynamic_slice_in_dim(grad_source, (1 - core) * rows_half, rows_half, axis=1)
    other = swapped(gone.astype(BF16), "rows", 1).astype(F32)
    images_grad = jnp.concatenate(
        [jnp.where(core == 0, top, other), jnp.where(core == 0, other, top)], axis=2
    )
    span = block_out.shape[4] // 2
    top = lax.dynamic_slice_in_dim(block_out, core * span, span, axis=4)
    gone = lax.dynamic_slice_in_dim(block_out, (1 - core) * span, span, axis=4)
    other = swapped(gone, "rows", 1)
    block_out = jnp.concatenate(
        [jnp.where(core == 0, top, other), jnp.where(core == 0, other, top)], axis=2
    )

    size = lax.axis_size("batch")

    def narrow(grad):
        return grad.astype(BF16).reshape(2, size, -1, 512)

    def by_core(grad):
        return jnp.swapaxes(grad.reshape(grad.shape[0], 2, -1), 0, 1)

    narrows = core_sum(
        jnp.concatenate(
            [
                narrow(grad_reduce_b),
                narrow(grad_squeeze_a),
                narrow(by_core(grad_excite_a)),
                narrow(grad_squeeze_b),
                narrow(by_core(grad_excite_b)),
            ],
            axis=2,
        ),
        0,
    )
    grads = (grad_expand_b, grad_spatial_b, grad_expand_a, grad_project_a, grad_spatial_a, grad_reduce_a)
    blocks = core_sum(jnp.concatenate([folded(grad) for grad in grads], axis=2), 1)
    summed = halved(jnp.concatenate([narrows, blocks], axis=1), two_orders)
    count = narrows.shape[1]
    gathered = collected(summed[:count].astype(BF16)).astype(F32)
    outs = []
    at = count
    for grad in grads:
        length = grad.size // (2 * size * 512)
        outs.append(unfolded(summed[at : at + length], grad.shape[1]))
        at += length
    out_expand_b, out_spatial_b, out_expand_a, out_project_a, out_spatial_a, out_reduce_a = outs
    unit = count // 8
    out_reduce_b = gathered[:, : 4 * unit].reshape(-1, mid)
    out_squeeze_a, out_excite_a, out_squeeze_b, out_excite_b = (
        gathered[:, k * unit : (k + 1) * unit] for k in range(4, 8)
    )
    small = all_sum(
        jnp.concatenate([small_one[0], small_one[1], small_two[0], small_two[1]]).reshape(-1, 128)
    ).reshape(-1)
    out = hid + vectors.shape[1]
    wide_out = vectors.shape[1]

    def own(vector):
        return lax.dynamic_slice_in_dim(vector, core * (wide_out // 2), wide_out // 2, axis=0)

    sums_all = [jnp.sum(s, axis=0) for s in (back_sums_one, back_sums_two, back_sums_four, back_sums_five)]
    three, side_sums, six = (
        jnp.sum(s, axis=0) for s in (back_sums_three[0], back_sums_three[1], back_sums_six)
    )
    return (
        block_out,
        images_grad,
        out_reduce_a,
        sums_all[0][1],
        sums_all[0][0],
        out_spatial_a,
        sums_all[1][1],
        sums_all[1][0],
        out_expand_a,
        own(three[1]),
        own(three[0]),
        out_project_a,
        own(side_sums[1]),
        own(side_sums[0]),
        out_squeeze_a.reshape(-1, hid),
        small[:hid],
        out_excite_a.reshape(hid, -1),
        own(small[hid:out]),
        out_reduce_b,
        sums_all[2][1],
        sums_all[2][0],
        out_spatial_b,
        sums_all[3][1],
        sums_all[3][0],
        out_expand_b,
        own(six[1]),
        own(six[0]),
        out_squeeze_b.reshape(-1, hid),
        small[out : out + hid],
        out_excite_b.reshape(hid, -1),
        own(small[out + hid :]),
    )


def solution(mesh):
    in_specs = (
        P(None, "rows", "batch", None, None),
        P(),
        P(),
        P(),
        P(),
        P(),
        P(),
        P(),
        P(),
        P("rows"),
        P("rows"),
        P(),
        P("rows"),
        P("rows"),
        P("rows", None),
        P(),
        P(None, "rows"),
        P("rows"),
        P("rows", None),
        P(),
        P(),
        P(),
        P(),
        P(),
        P(),
        P("rows"),
        P("rows"),
        P("rows", None),
        P(),
        P(None, "rows"),
        P("rows"),
        P(None, None, "batch", None, "rows"),
    )
    out_specs = (
        P(None, None, "batch", None, "rows"),
        P(None, "rows", "batch", None, None),
        P(("batch", "rows")),
        P(),
        P(),
        P(("batch", "rows")),
        P(),
        P(),
        P(("batch", "rows")),
        P("rows"),
        P("rows"),
        P(("batch", "rows")),
        P("rows"),
        P("rows"),
        P("rows", None),
        P(),
        P(None, "rows"),
        P("rows"),
        P("rows", None),
        P(),
        P(),
        P(("batch", "rows")),
        P(),
        P(),
        P(("batch", "rows")),
        P("rows"),
        P("rows"),
        P("rows", None),
        P(),
        P(None, "rows"),
        P("rows"),
    )
    return jax.shard_map(
        per_device, mesh=mesh, in_specs=in_specs, out_specs=out_specs, check_vma=False
    )
```

time: 2220 us -> 755 us (0.34)
  blocking collectives: 758 us -> 56.4 us
  local copies, waits for them, and re-layouts: 563 us -> 131 us
  waiting for transfers between devices: 580 us -> 292 us
  matrix products: 134 us -> 91.6 us
  starting transfers between devices: 35.8 us -> 63 us
    psum x17 -> x0, blocking collectives: 704 us -> none  [the longest x5 373 us: channel_total(): return lax.psum((first, second), 'batch')]
    unnamed x5 -> x0, waiting for transfers between devices: 554 us -> none
    unnamed x784 -> x327, local copies, waits for them, and re-layouts: 224 us -> 37.3 us
    ppermute x12 -> x34, waiting for transfers between devices: 0.03 us -> 180 us  [swapped(): return lax.ppermute(block, axis, route)]
    pad x18 -> x0, local copies, waits for them, and re-layouts: 136 us -> none  [gather_taps(): padded[row_tap:row_tap + stride * out_rows:stride, :, col_tap:col_tap + s...]
    convert_element_type x12 -> x5, local copies, waits for them, and re-layouts: 140 us -> 6.07 us  [the longest x4 3.61 us: narrow(): return grad.astype(BF16).reshape(2, size, -1, 512)]
    all_to_all x2 -> x9, waiting for transfers between devices: 0.01 us -> 113 us  [all_sum(): return jnp.sum(lax.all_to_all(spread, 'batch', 0, 0, tiled=True), axis=0)]
    all_to_all x2 -> x9, starting transfers between devices: 7.7 us -> 49.7 us  [all_sum(): return jnp.sum(lax.all_to_all(spread, 'batch', 0, 0, tiled=True), axis=0)]
  transfers between devices with their start and end apart: 18 -> 43, of which waited for: 3 -> 26; matrix products, arithmetic and copies ran while one was open for 16% -> 20% of each run, Pallas kernels for 0% -> 0%
where the time goes in v1:
time: 755 us; the launch traced here: 743 us
  waiting for transfers between devices  292 us (39%)
  local copies, waits for them, and re-layouts  131 us (17%)
  other arithmetic  104 us (14%)
  matrix products  91.6 us (12%)
  starting transfers between devices  63 us (8%)
  blocking collectives  56.4 us (7%)
    ppermute x34, waiting for transfers between devices, swapped(): return lax.ppermute(block, axis, route)  180 us
    all_to_all x9, waiting for transfers between devices, all_sum(): return jnp.sum(lax.all_to_all(spread, 'batch', 0, 0, tiled=True), axis=0)  113 us
    all_to_all x4, blocking collectives, all_sum(): return jnp.sum(lax.all_to_all(spread, 'batch', 0, 0, tiled=True), axis=0)  56.4 us
    all_to_all x9, starting transfers between devices, all_sum(): return jnp.sum(lax.all_to_all(spread, 'batch', 0, 0, tiled=True), axis=0)  49.7 us
    unnamed x327, local copies, waits for them, and re-layouts  37.3 us
    dot_general x23, matrix products, input_dot(): lax.dot_general(grads, weight, (((grads.ndim - 1,), (1,)), ((), ())), pre...  28 us
    dot_general x7, matrix products, forward_dot(): return jnp.dot(inputs, weight, preferred_element_type=F32)  26.1 us
    dot_general x7, matrix products, weight_dot(): lax.dot_general(inputs, grads, ((leading, leading), ((), ())), preferred_...  18.1 us
  transfers between devices with their start and end apart: 43, of which 26 were waited for; matrix products, arithmetic and copies ran while one was open for 20% of the time, Pallas kernels for 0%

profile of v1, /device:TPU:0, one launch (start us, length us, event | category | flops | bytes accessed | tf_op | source)
XLA Modules:
  0.0 742.7 jit_solution(11531048670690548797)
XLA Ops:
  18.5 8.0 %all-to-all-start = ((f32[16,2,2,512]{3,2,1,0:T(2,128)}), f32[16,2,2,512]{3,2,1,0:T(2,128)S(1)}, u32[]{:S(2)}, u32[]{:S(2)}) async-start(f32[16,2,2,512]{3,2,1,0:T(2,128)} %broadcast_in_dim.32), calls=%async_computation | async-start | bytes 262144 | tf_op jit(solution)/shard_map/all_to_all | solution.py:27
  26.8 7.7 %all-to-all-done = f32[16,2,2,512]{3,2,1,0:T(2,128)S(1)} async-done(((f32[16,2,2,512]{3,2,1,0:T(2,128)}), f32[16,2,2,512]{3,2,1,0:T(2,128)S(1)}, u32[]{:S(2)}, u32[]{:S(2)}) %all-to-all-start) | async-done | bytes 131104 | tf_op jit(solution)/shard_map/all_to_all | solution.py:27
  38.1 5.4 multiply_reduce_fusion.7
  84.2 11.0 %all-to-all-done.2 = f32[16,2,2,2,2048]{4,3,2,1,0:T(2,128)} async-done(((f32[16,2,2,2,2048]{4,3,2,1,0:T(2,128)}), f32[16,2,2,2,2048]{4,3,2,1,0:T(2,128)}, u32[]{:S(2)}, u32[]{:S(2)}) %all-to-all-start.2) | async-done | bytes 1048608 | tf_op jit(solution)/shard_map/all_to_all | solution.py:27
  106.8 14.4 %all_to_all.65 = f32[16,2,2,512]{3,2,1,0:T(2,128)S(1)} all-to-all(f32[16,2,2,512]{3,2,1,0:T(2,128)S(1)} %broadcast_in_dim.35), channel_id=1, replica_groups=mesh['batch'=16,'rows'=2] {'batch'}, dimensions={0} | all-to-all | bytes 262144 | tf_op jit(solution)/shard_map/all_to_all | solution.py:27
  125.5 5.4 multiply_reduce_fusion.5
  132.2 11.1 %all_to_all.66 = f32[16,2,2,512]{3,2,1,0:T(2,128)S(1)} all-to-all(f32[16,2,2,512]{3,2,1,0:T(2,128)S(1)} %broadcast_in_dim.36), channel_id=1, replica_groups=mesh['batch'=16,'rows'=2] {'batch'}, dimensions={0} | all-to-all | bytes 262144 | tf_op jit(solution)/shard_map/all_to_all | solution.py:27
  160.4 10.2 %all-to-all-done.5 = f32[16,2,2,2048]{3,2,1,0:T(2,128)} async-done(((f32[16,2,2,2048]{3,2,1,0:T(2,128)}), f32[16,2,2,2048]{3,2,1,0:T(2,128)}, u32[]{:S(2)}, u32[]{:S(2)}) %all-to-all-start.5) | async-done | bytes 524320 | tf_op jit(solution)/shard_map/all_to_all | solution.py:27
  189.1 19.3 %all_to_all.67 = f32[16,2,2,2048]{3,2,1,0:T(2,128)S(1)} all-to-all(f32[16,2,2,2048]{3,2,1,0:T(2,128)S(1)} %broadcast_in_dim.38), channel_id=1, replica_groups=mesh['batch'=16,'rows'=2] {'batch'}, dimensions={0} | all-to-all | bytes 1048576 | tf_op jit(solution)/shard_map/all_to_all | solution.py:27
  213.6 11.5 %all_to_all.68 = f32[16,2,2,512]{3,2,1,0:T(2,128)S(1)} all-to-all(f32[16,2,2,512]{3,2,1,0:T(2,128)S(1)} %broadcast_in_dim.39), channel_id=1, replica_groups=mesh['batch'=16,'rows'=2] {'batch'}, dimensions={0} | all-to-all | bytes 262144 | tf_op jit(solution)/shard_map/all_to_all | solution.py:27
  255.5 6.8 multiply_reduce_fusion.2
  275.6 6.9 all-to-all-start.9
  288.2 19.2 %all-to-all-done.9 = f32[16,2,2,2,2048]{4,3,2,1,0:T(2,128)} async-done(((f32[16,2,2,2,2048]{4,3,2,1,0:T(2,128)}), f32[16,2,2,2,2048]{4,3,2,1,0:T(2,128)}, u32[]{:S(2)}, u32[]{:S(2)}) %all-to-all-start.9) | async-done | bytes 1048608 | tf_op jit(solution)/shard_map/all_to_all | solution.py:27
  313.4 4.8 bitcast_convert_fusion.2
  326.0 7.1 all-to-all-start.10
  334.7 7.8 %reshape.1204 = bf16[16,2,32,4,512]{4,3,2,1,0:T(4,128)(2,1)} reshape(bf16[1024,2048]{1,0:T(8,128)(2,1)} %bitcast_convert_fusion.2) | data formatting | bytes 8388608 | tf_op jit(solution)/shard_map/reshape | solution.py:166
  369.4 7.3 all-to-all-start.11
  376.7 5.0 copy_dynamic-update-slice_fusion
  389.3 8.2 %dynamic-slice_bitcast_fusion = bf16[16,576,512]{2,1,0:T(8,128)(2,1)} fusion(bf16[16,2,576,512]{3,2,0,1:T(8,128)(2,1)} %copy_dynamic-update-slice_fusion.2, s32[]{:T(128)S(6)} %select_n.297), kind=kLoop, calls=%fused_computation.5 | loop fusion | bytes 18874372 | tf_op jit(solution)/shard_map/jit(dynamic_index_in_dim)/squeeze | solution.py:69
  421.4 7.8 %fusion = bf16[16,576,512]{2,1,0:T(8,128)(2,1)S(1)} fusion(bf16[16,576,512]{2,1,0:T(8,128)(2,1)} %collective-permute-done.19, bf16[16,2,576,512]{3,2,0,1:T(8,128)(2,1)} %copy_dynamic-update-slice_fusion.2, s32[]{:T(128)S(6)} %select_n.296), kind=kLoop, calls=%fused_computation.2 | loop fusion | flops 18874368 | bytes 28311556 | tf_op jit(solution)/shard_map/convert_element_type | solution.py:71
  429.2 5.0 pad_maximum_fusion
  448.0 58.6 %all-to-all-done.12 = f32[16,34,128]{2,1,0:T(8,128)S(1)} async-done(((f32[16,34,128]{2,1,0:T(8,128)}), f32[16,34,128]{2,1,0:T(8,128)S(1)}, u32[]{:S(2)}, u32[]{:S(2)}) %all-to-all-start.12) | async-done | bytes 278560 | tf_op jit(solution)/shard_map/all_to_all | solution.py:27
  523.3 82.4 %collective-permute-done.26 = bf16[2,2,352,512]{3,2,0,1:T(8,128)(2,1)S(1)} collective-permute-done((bf16[2,2,352,512]{3,2,0,1:T(8,128)(2,1)S(1)}, bf16[2,2,352,512]{3,2,0,1:T(8,128)(2,1)S(1)}, u32[]{:S(2)}, u32[]{:S(2)}) %collective-permute-start.26) | collective-permute-done | bytes 1441824 | tf_op jit(solution)/shard_map/ppermute | solution.py:16
  612.0 5.3 copy.274
  617.4 10.4 %scatter_fusion = f32[2,16,2,16,1024]{4,2,3,1,0:T(2,128)} fusion(f32[2,16,2,16,1024]{4,2,3,1,0:T(2,128)} %copy.274, s32[64]{0:T(128)S(1)} %reshape.1236, f32[64,2,2,1024]{3,2,1,0:T(2,128)S(1)} %copy.275), kind=kCustom, calls=%fused_computation | custom fusion | flops 262144 | bytes 3146240 | tf_op jit(solution)/shard_map/scatter-add | solution.py:439
  634.5 12.2 %collective-permute-done.28 = bf16[352,512]{1,0:T(8,128)(2,1)S(1)} collective-permute-done((bf16[352,512]{1,0:T(8,128)(2,1)S(1)}, bf16[352,512]{1,0:T(8,128)(2,1)S(1)}, u32[]{:S(2)}, u32[]{:S(2)}) %collective-permute-start.28) | collective-permute-done | bytes 360480 | tf_op jit(solution)/shard_map/ppermute | solution.py:16
  653.7 4.6 collective-permute-done.30
  661.1 5.3 copy.296
  666.4 6.4 collective-permute-done.22
  673.1 10.0 %collective-permute-done.31 = bf16[4,128,512]{2,1,0:T(8,128)(2,1)S(1)} collective-permute-done((bf16[4,128,512]{2,1,0:T(8,128)(2,1)S(1)}, bf16[4,128,512]{2,1,0:T(8,128)(2,1)S(1)}, u32[]{:S(2)}, u32[]{:S(2)}) %collective-permute-start.31) | collective-permute-done | bytes 524320 | tf_op jit(solution)/shard_map/ppermute | solution.py:16
  684.2 29.2 %collective-permute-done.23 = bf16[352,512]{1,0:T(8,128)(2,1)S(1)} collective-permute-done((bf16[352,512]{1,0:T(8,128)(2,1)S(1)}, bf16[352,512]{1,0:T(8,128)(2,1)S(1)}, u32[]{:S(2)}, u32[]{:S(2)}) %collective-permute-start.23) | collective-permute-done | bytes 360480 | tf_op jit(solution)/shard_map/ppermute | solution.py:16
  717.6 15.7 %collective-permute-done.32 = bf16[8,128,512]{2,1,0:T(8,128)(2,1)S(1)} collective-permute-done((bf16[8,128,512]{2,1,0:T(8,128)(2,1)S(1)}, bf16[8,128,512]{2,1,0:T(8,128)(2,1)S(1)}, u32[]{:S(2)}, u32[]{:S(2)}) %collective-permute-start.32) | collective-permute-done | bytes 1048608 | tf_op jit(solution)/shard_map/ppermute | solution.py:16
  (696 shorter events, 308.2 us)
Async XLA Ops:
  4.6 3.1 collective-permute-start
  18.5 16.0 %all-to-all-start = ((f32[16,2,2,512]{3,2,1,0:T(2,128)}), f32[16,2,2,512]{3,2,1,0:T(2,128)S(1)}, u32[]{:S(2)}, u32[]{:S(2)}) async-start(f32[16,2,2,512]{3,2,1,0:T(2,128)} %broadcast_in_dim.32), calls=%async_computation | async-start | bytes 262144 | tf_op jit(solution)/shard_map/all_to_all | solution.py:27
  43.6 3.1 collective-permute-start.2
  47.4 11.9 %all-to-all-start.1 = ((f32[16,2,2,512]{3,2,1,0:T(2,128)}), f32[16,2,2,512]{3,2,1,0:T(2,128)S(1)}, u32[]{:S(2)}, u32[]{:S(2)}) async-start(f32[16,2,2,512]{3,2,1,0:T(2,128)} %broadcast_in_dim.33), calls=%async_computation.1 | async-start | bytes 262144 | tf_op jit(solution)/shard_map/all_to_all | solution.py:27
  64.0 15.4 %collective-permute-start.5 = (bf16[1024,768]{1,0:T(8,128)(2,1)}, bf16[1024,768]{1,0:T(8,128)(2,1)}, u32[]{:S(2)}, u32[]{:S(2)}) collective-permute-start(bf16[1024,768]{1,0:T(8,128)(2,1)} %constant_dynamic-update-slice_fusion.3), channel_id=1, source_target_pairs={{0,1},{1,0},{2,3},{3,2},{4,5},{5,4},{6,7},{7,6},{8,9},{9,8},{10,11... | collective-permute-start | bytes 4718600 | tf_op jit(solution)/shard_map/ppermute | solution.py:16
  66.1 29.0 %all-to-all-start.2 = ((f32[16,2,2,2,2048]{4,3,2,1,0:T(2,128)}), f32[16,2,2,2,2048]{4,3,2,1,0:T(2,128)}, u32[]{:S(2)}, u32[]{:S(2)}) async-start(f32[16,2,2,2,2048]{4,3,2,1,0:T(2,128)} %broadcast_in_dim.34), calls=%async_computation.2 | async-start | bytes 2097152 | tf_op jit(solution)/shard_map/all_to_all | solution.py:27
  73.8 2.6 collective-permute-start.6
  150.9 19.7 %all-to-all-start.5 = ((f32[16,2,2,2048]{3,2,1,0:T(2,128)}), f32[16,2,2,2048]{3,2,1,0:T(2,128)}, u32[]{:S(2)}, u32[]{:S(2)}) async-start(f32[16,2,2,2048]{3,2,1,0:T(2,128)} %broadcast_in_dim.37), calls=%async_computation.5 | async-start | bytes 1048576 | tf_op jit(solution)/shard_map/all_to_all | solution.py:27
  156.3 2.0 collective-permute-start.11
  235.7 16.1 %all-to-all-start.8 = ((f32[16,2,2,512]{3,2,1,0:T(2,128)}), f32[16,2,2,512]{3,2,1,0:T(2,128)}, u32[]{:S(2)}, u32[]{:S(2)}) async-start(f32[16,2,2,512]{3,2,1,0:T(2,128)} %broadcast_in_dim.40), calls=%async_computation.8 | async-start | bytes 262144 | tf_op jit(solution)/shard_map/all_to_all | solution.py:27
  275.6 31.7 %all-to-all-start.9 = ((f32[16,2,2,2,2048]{4,3,2,1,0:T(2,128)}), f32[16,2,2,2,2048]{4,3,2,1,0:T(2,128)}, u32[]{:S(2)}, u32[]{:S(2)}) async-start(f32[16,2,2,2,2048]{4,3,2,1,0:T(2,128)} %broadcast_in_dim.41), calls=%async_computation.9 | async-start | bytes 2097152 | tf_op jit(solution)/shard_map/all_to_all | solution.py:27
  319.2 6.1 collective-permute-start.16
  326.0 22.5 %all-to-all-start.10 = ((f32[16,2,2,512]{3,2,1,0:T(2,128)}), f32[16,2,2,512]{3,2,1,0:T(2,128)S(1)}, u32[]{:S(2)}, u32[]{:S(2)}) async-start(f32[16,2,2,512]{3,2,1,0:T(2,128)} %broadcast_in_dim.42), calls=%async_computation.10 | async-start | bytes 262144 | tf_op jit(solution)/shard_map/all_to_all | solution.py:27
  364.9 3.9 collective-permute-start.17
  369.4 14.9 %all-to-all-start.11 = ((f32[16,2,2,512]{3,2,1,0:T(2,128)}), f32[16,2,2,512]{3,2,1,0:T(2,128)S(1)}, u32[]{:S(2)}, u32[]{:S(2)}) async-start(f32[16,2,2,512]{3,2,1,0:T(2,128)} %broadcast_in_dim.43), calls=%async_computation.11 | async-start | bytes 262144 | tf_op jit(solution)/shard_map/all_to_all | solution.py:27
  397.5 23.9 %collective-permute-start.19 = (bf16[16,576,512]{2,1,0:T(8,128)(2,1)}, bf16[16,576,512]{2,1,0:T(8,128)(2,1)}, u32[]{:S(2)}, u32[]{:S(2)}) collective-permute-start(bf16[16,576,512]{2,1,0:T(8,128)(2,1)} %dynamic-slice_bitcast_fusion), channel_id=1, source_target_pairs={{0,1},{1,0},{2,3},{3,2},{4,5},{5,4},{6,7},{7,6},{8,9},{9,8},{10,11... | collective-permute-start | bytes 28311560 | tf_op jit(solution)/shard_map/ppermute | solution.py:16
  413.1 5.4 collective-permute-start.24
  413.6 4.4 collective-permute-start.10
  438.1 76.1 %collective-permute-start.25 = (bf16[2,2,2,352,512]{4,3,0,1,2:T(8,128)(2,1)}, bf16[2,2,2,352,512]{4,3,0,1,2:T(8,128)(2,1)}, u32[]{:S(2)}, u32[]{:S(2)}) collective-permute-start(bf16[2,2,2,352,512]{4,3,0,1,2:T(8,128)(2,1)} %bitcast.619), channel_id=1, source_target_pairs={{0,2},{2,0},{4,6},{6,4},{8,10},{10,8},{12,14},{14,12},{16,18},{18,... | collective-permute-start | bytes 8650760 | tf_op jit(solution)/shard_map/ppermute | solution.py:16
  442.5 64.2 %all-to-all-start.12 = ((f32[16,34,128]{2,1,0:T(8,128)}), f32[16,34,128]{2,1,0:T(8,128)S(1)}, u32[]{:S(2)}, u32[]{:S(2)}) async-start(f32[16,34,128]{2,1,0:T(8,128)} %broadcast_in_dim.47), calls=%async_computation.12 | async-start | bytes 655360 | tf_op jit(solution)/shard_map/all_to_all | solution.py:27
  510.7 97.1 %collective-permute-start.20 = (bf16[2,2,2,352,512]{4,3,2,1,0:T(8,128)(2,1)S(1)}, bf16[2,2,2,352,512]{4,3,2,1,0:T(8,128)(2,1)S(1)}, u32[]{:S(2)}, u32[]{:S(2)}) collective-permute-start(bf16[2,2,2,352,512]{4,3,2,1,0:T(8,128)(2,1)S(1)} %dynamic-slice_bitcast_fusion.1), channel_id=1, source_target_pairs={{0,4},{2,6},{4,0},{6,2},{8,12},{10,14},{12,8},{14,10},{16,20},{18,... | collective-permute-start | bytes 8650760 | tf_op jit(solution)/shard_map/ppermute | solution.py:16
  518.2 87.6 %collective-permute-start.26 = (bf16[2,2,352,512]{3,2,0,1:T(8,128)(2,1)S(1)}, bf16[2,2,352,512]{3,2,0,1:T(8,128)(2,1)S(1)}, u32[]{:S(2)}, u32[]{:S(2)}) collective-permute-start(bf16[2,2,352,512]{3,2,0,1:T(8,128)(2,1)S(1)} %dynamic-slice_bitcast_fusion.3), channel_id=1, source_target_pairs={{0,4},{2,6},{4,0},{6,2},{8,12},{10,14},{12,8},{14,10},{16,20},{18,... | collective-permute-start | bytes 4325384 | tf_op jit(solution)/shard_map/ppermute | solution.py:16
  607.1 20.7 %collective-permute-start.27 = (bf16[2,352,512]{2,1,0:T(8,128)(2,1)}, bf16[2,352,512]{2,1,0:T(8,128)(2,1)}, u32[]{:S(2)}, u32[]{:S(2)}) collective-permute-start(bf16[2,352,512]{2,1,0:T(8,128)(2,1)} %dynamic-slice_bitcast_fusion.5), channel_id=1, source_target_pairs={{0,8},{2,10},{4,12},{6,14},{8,0},{10,2},{12,4},{14,6},{16,24},{18,... | collective-permute-start | bytes 2162696 | tf_op jit(solution)/shard_map/ppermute | solution.py:16
  609.9 37.9 %collective-permute-start.21 = (bf16[2,2,352,512]{3,2,1,0:T(8,128)(2,1)}, bf16[2,2,352,512]{3,2,1,0:T(8,128)(2,1)}, u32[]{:S(2)}, u32[]{:S(2)}) collective-permute-start(bf16[2,2,352,512]{3,2,1,0:T(8,128)(2,1)} %dynamic-slice_bitcast_fusion.4), channel_id=1, source_target_pairs={{0,2},{2,0},{4,6},{6,4},{8,10},{10,8},{12,14},{14,12},{16,18},{18,... | collective-permute-start | bytes 4325384 | tf_op jit(solution)/shard_map/ppermute | solution.py:16
  629.2 17.5 %collective-permute-start.28 = (bf16[352,512]{1,0:T(8,128)(2,1)S(1)}, bf16[352,512]{1,0:T(8,128)(2,1)S(1)}, u32[]{:S(2)}, u32[]{:S(2)}) collective-permute-start(bf16[352,512]{1,0:T(8,128)(2,1)S(1)} %dynamic-slice_bitcast_fusion.7), channel_id=1, source_target_pairs={{0,16},{2,18},{4,20},{6,22},{8,24},{10,26},{12,28},{14,30},{16,0},... | collective-permute-start | bytes 1081352 | tf_op jit(solution)/shard_map/ppermute | solution.py:16
  633.8 18.4 %collective-permute-start.18 = (bf16[2,8,2,16,1024]{4,2,3,1,0:T(2,128)(2,1)S(1)}, bf16[2,8,2,16,1024]{4,2,3,1,0:T(2,128)(2,1)S(1)}, u32[]{:S(2)}, u32[]{:S(2)}) collective-permute-start(bf16[2,8,2,16,1024]{4,2,3,1,0:T(2,128)(2,1)S(1)} %dynamic-slice_convert_fusion), channel_id=1, source_target_pairs={{0,1},{1,0},{2,3},{3,2},{4,5},{5,4},{6,7},{7,6},{8,9},{9,8},{10,11... | collective-permute-start | bytes 3145736 | tf_op jit(solution)/shard_map/ppermute | solution.py:16
  646.8 5.0 collective-permute-start.29
  649.8 23.0 %collective-permute-start.22 = (bf16[2,352,512]{2,1,0:T(8,128)(2,1)S(1)}, bf16[2,352,512]{2,1,0:T(8,128)(2,1)S(1)}, u32[]{:S(2)}, u32[]{:S(2)}) collective-permute-start(bf16[2,352,512]{2,1,0:T(8,128)(2,1)S(1)} %dynamic-slice_bitcast_fusion.6), channel_id=1, source_target_pairs={{0,8},{2,10},{4,12},{6,14},{8,0},{10,2},{12,4},{14,6},{16,24},{18,... | collective-permute-start | bytes 2162696 | tf_op jit(solution)/shard_map/ppermute | solution.py:16
  651.9 6.4 collective-permute-start.30
  658.4 24.7 %collective-permute-start.31 = (bf16[4,128,512]{2,1,0:T(8,128)(2,1)S(1)}, bf16[4,128,512]{2,1,0:T(8,128)(2,1)S(1)}, u32[]{:S(2)}, u32[]{:S(2)}) collective-permute-start(bf16[4,128,512]{2,1,0:T(8,128)(2,1)S(1)} %pad_maximum_fusion.8), channel_id=1, source_target_pairs={{0,8},{2,10},{4,12},{6,14},{8,0},{10,2},{12,4},{14,6},{16,24},{18,... | collective-permute-start | bytes 1572872 | tf_op jit(solution)/shard_map/ppermute | solution.py:16
  673.0 40.4 %collective-permute-start.23 = (bf16[352,512]{1,0:T(8,128)(2,1)S(1)}, bf16[352,512]{1,0:T(8,128)(2,1)S(1)}, u32[]{:S(2)}, u32[]{:S(2)}) collective-permute-start(bf16[352,512]{1,0:T(8,128)(2,1)S(1)} %dynamic-slice_bitcast_fusion.8), channel_id=1, source_target_pairs={{0,16},{2,18},{4,20},{6,22},{8,24},{10,26},{12,28},{14,30},{16,0},... | collective-permute-start | bytes 1081352 | tf_op jit(solution)/shard_map/ppermute | solution.py:16
  683.3 50.0 %collective-permute-start.32 = (bf16[8,128,512]{2,1,0:T(8,128)(2,1)S(1)}, bf16[8,128,512]{2,1,0:T(8,128)(2,1)S(1)}, u32[]{:S(2)}, u32[]{:S(2)}) collective-permute-start(bf16[8,128,512]{2,1,0:T(8,128)(2,1)S(1)} %pad_maximum_fusion.4), channel_id=1, source_target_pairs={{0,16},{2,18},{4,20},{6,22},{8,24},{10,26},{12,28},{14,30},{16,0},... | collective-permute-start | bytes 3145736 | tf_op jit(solution)/shard_map/ppermute | solution.py:16
  (154 other events, 1928.9 us)
